TPU v7x, 512 devices: a whole 4x8x8 slice. The times are simulated.
512 devices in a mesh: dp: 64 (over z, x, y_lo), node: 8 (over y_hi, core).
Axes of the slice: x: 4, y: 8 (y_hi: 4, y_lo: 2; y = y_hi * 2 + y_lo), z: 8, core: 2. Of those that a mesh axis runs over, the one named last changes fastest.
Arguments:
- tokens: bfloat16 [1536, 5120], P('node'), may hold values from -6 to 6
- cotangent: bfloat16 [1536, 5120], P('node'), may hold values from -6 to 6
- gate_codes: bfloat16 [5120, 8192], P('node', 'dp'), may hold values from -16 to 16
- up_codes: bfloat16 [5120, 8192], P('node', 'dp'), may hold values from -16 to 16
- down_codes: bfloat16 [8192, 5120], P('dp', 'node'), may hold values from -4 to 4
- gate_scales: float32 [40, 8192], P(None, 'dp'), may hold values from 0.00559017 to 0.034938563
- up_scales: float32 [40, 8192], P(None, 'dp'), may hold values from 0.00559017 to 0.034938563
- down_scales: float32 [8192, 40], P('dp'), may hold values from 0.0044194176 to 0.027621359
Outputs:
- token_grad: bfloat16 [1536, 5120], P('node', 'dp')
- gate_grad: bfloat16 [5120, 8192], P('node', 'dp')
- up_grad: bfloat16 [5120, 8192], P('node', 'dp')
- down_grad: bfloat16 [8192, 5120], P('dp', 'node')
All inputs are finite; a program needn't handle non-finite values.
Results may differ from a plain program's by a relative error of at most 0.0077.
Values may be sent and summed in bfloat16 or wider, within the bound.
A program may use at most 64 MiB of HBM per device.

v0:
```python
import jax
import jax.numpy as jnp
from jax import lax
from jax.sharding import PartitionSpec as P

QB = 128


def shortened(value):
    return jax.tree.map(lambda a: a.astype(jnp.bfloat16) if a.dtype == jnp.float32 else a, value)


def scale_rows(codes, scales):
    blocks = codes.astype(jnp.float32).reshape(scales.shape[0], QB, codes.shape[1])
    return (blocks * scales[:, None, :]).reshape(codes.shape).astype(jnp.bfloat16)


def contract(left, right):
    return lax.dot_general(
        left, right, (((0,), (0,)), ((), ())), preferred_element_type=jnp.float32
    )


def against(left, right):
    return lax.dot_general(
        left, right, (((1,), (1,)), ((), ())), preferred_element_type=jnp.float32
    )


def body(tokens, cotangent, gate_codes, up_codes, down_codes, gate_scales, up_scales, down_scales):
    node_count = lax.axis_size("node")
    full_codes = (
        lax.all_gather(gate_codes, "node", axis=0, tiled=True),
        lax.all_gather(up_codes, "node", axis=0, tiled=True),
        lax.all_gather(down_codes, "node", axis=1, tiled=True),
    )
    w_gate = scale_rows(full_codes[0], gate_scales)
    w_up = scale_rows(full_codes[1], up_scales)
    w_down_t = scale_rows(full_codes[2].T, down_scales.T)
    gate = jnp.dot(tokens, w_gate, preferred_element_type=jnp.float32)
    upper = jnp.dot(tokens, w_up, preferred_element_type=jnp.float32)
    sig = jax.nn.sigmoid(gate)
    silu_val = gate * sig
    act = (silu_val * upper).astype(jnp.bfloat16)
    d_act = jnp.dot(cotangent, w_down_t, preferred_element_type=jnp.float32)
    d_gate = (d_act * upper * sig * (1.0 + gate * (1.0 - sig))).astype(jnp.bfloat16)
    d_up = (d_act * silu_val).astype(jnp.bfloat16)
    token_terms = against(d_gate, w_gate) + against(d_up, w_up)
    token_grad = lax.psum_scatter(token_terms, "dp", scatter_dimension=1, tiled=True).astype(
        jnp.bfloat16
    )
    width = d_gate.shape[1]
    partials = (contract(tokens, d_gate), contract(tokens, d_up), contract(cotangent, act))
    rounded = tuple((p.astype(jnp.bfloat16).reshape(node_count, -1, width) for p in partials))
    received = jax.tree.map(
        lambda part, own: part.astype(own.dtype),
        lax.all_to_all(shortened(rounded), "node", split_axis=0, concat_axis=0, tiled=True),
        rounded,
    )
    sums = tuple((r.astype(jnp.float32).sum(axis=0).astype(jnp.bfloat16) for r in received))
    return (token_grad, sums[0], sums[1], sums[2].T)


def solution(mesh):
    return jax.shard_map(
        body,
        mesh=mesh,
        in_specs=(
            P("node", None),
            P("node", None),
            P("node", "dp"),
            P("node", "dp"),
            P("dp", "node"),
            P(None, "dp"),
            P(None, "dp"),
            P("dp", None),
        ),
        out_specs=(P("node", "dp"), P("node", "dp"), P("node", "dp"), P("dp", "node")),
        check_vma=False,
    )
```

profile of v0, /device:TPU:16, one launch (start us, length us, event | category | flops | bytes accessed | tf_op | source)
XLA Modules:
  0.0 499.6 jit_solution(1077485587360639443)
XLA Ops:
  7.2 0.0 copy-start
  7.2 0.0 copy-start.6
  7.2 0.0 all-gather.8.cloned.1.call-start
  7.2 0.7 all-gather.8.cloned.1.call-update
  7.9 0.0 all-gather.6.cloned.1.call-start
  8.0 0.7 all-gather.6.cloned.1.call-update
  8.7 0.0 all-gather.4.cloned.1.call-start
  8.7 0.7 all-gather.4.cloned.1.call-update
  9.4 0.0 reduce-scatter.2.cloned.1.call-start
  9.5 0.8 copy.13
  10.3 37.2 %all-gather.8.cloned.1.call-done = bf16[5120,128]{1,0:T(8,128)(2,1)} async-done(((bf16[640,128]{1,0:T(8,128)(2,1)}), bf16[5120,128]{1,0:T(8,128)(2,1)}) %all-gather.8.cloned.1.call-update) | async-done | bytes 1310736 | tf_op jit(solution)/shard_map/all_gather | solution.py:33
  47.5 1.6 fusion.1
  49.1 33.4 %all-gather.6.cloned.1.call-done = bf16[5120,128]{1,0:T(8,128)(2,1)} async-done(((bf16[640,128]{1,0:T(8,128)(2,1)}), bf16[5120,128]{1,0:T(8,128)(2,1)}) %all-gather.6.cloned.1.call-update) | async-done | bytes 1310736 | tf_op jit(solution)/shard_map/all_gather | solution.py:34
  82.4 0.0 copy-done.6
  82.4 1.6 fusion.2
  84.0 0.0 copy-done
  84.0 0.0 copy-start.1
  84.0 0.7 convolution_bitcast_fusion
  84.7 0.4 copy-done.1
  85.1 0.7 convolution_bitcast_fusion.1
  85.8 31.9 %all-gather.4.cloned.1.call-done = bf16[128,5120]{1,0:T(8,128)(2,1)} async-done(((bf16[128,640]{1,0:T(8,128)(2,1)}), bf16[128,5120]{1,0:T(8,128)(2,1)}) %all-gather.4.cloned.1.call-update) | async-done | bytes 1310736 | tf_op jit(solution)/shard_map/all_gather | solution.py:35
  117.7 0.0 copy-start.3
  117.7 0.7 mul.54
  118.5 0.8 copy-done.3
  119.3 2.2 multiply_convert_fusion.1
  121.4 0.0 copy-start.4
  121.5 0.0 copy-start.2
  121.5 0.9 fusion.11
  122.3 0.0 copy-done.4
  122.3 0.5 copy-done.2
  122.8 3.2 convolution_add_fusion
  126.0 0.0 copy-start.5
  126.0 0.0 reduce-scatter.2.cloned.1.call-update
  126.0 0.8 copy-done.5
  126.8 0.5 convolution_convert_fusion.2
  127.3 1.2 copy.38
  128.5 5.5 %all-to-all-start = ((bf16[8,640,128]{1,2,0:T(8,128)(2,1)}), bf16[8,640,128]{1,2,0:T(8,128)(2,1)S(1)}, u32[]{:S(2)}, u32[]{:S(2)}) async-start(bf16[8,640,128]{1,2,0:T(8,128)(2,1)} %bitcast.69), calls=%async_computation.1 | async-start | bytes 2621440 | tf_op jit(solution)/shard_map/all_to_all | solution.py:57
  134.0 0.5 convolution_convert_fusion.1
  134.6 1.2 copy.37
  135.7 37.4 %all-to-all-done = bf16[8,640,128]{1,2,0:T(8,128)(2,1)S(1)} async-done(((bf16[8,640,128]{1,2,0:T(8,128)(2,1)}), bf16[8,640,128]{1,2,0:T(8,128)(2,1)S(1)}, u32[]{:S(2)}, u32[]{:S(2)}) %all-to-all-start) | async-done | bytes 1310752 | tf_op jit(solution)/shard_map/all_to_all | solution.py:57
  173.1 6.1 %all-to-all-start.1 = ((bf16[8,640,128]{1,2,0:T(8,128)(2,1)}), bf16[8,640,128]{1,2,0:T(8,128)(2,1)}, u32[]{:S(2)}, u32[]{:S(2)}) async-start(bf16[8,640,128]{1,2,0:T(8,128)(2,1)} %bitcast.68), calls=%async_computation.2 | async-start | bytes 2621440 | tf_op jit(solution)/shard_map/all_to_all | solution.py:57
  179.2 2.1 convolution_convert_fusion
  181.3 1.3 copy.36
  182.6 38.8 %all-to-all-done.1 = bf16[8,640,128]{1,2,0:T(8,128)(2,1)} async-done(((bf16[8,640,128]{1,2,0:T(8,128)(2,1)}), bf16[8,640,128]{1,2,0:T(8,128)(2,1)}, u32[]{:S(2)}, u32[]{:S(2)}) %all-to-all-start.1) | async-done | bytes 1310752 | tf_op jit(solution)/shard_map/all_to_all | solution.py:57
  221.4 7.4 %all-to-all-start.2 = ((bf16[8,640,128]{1,2,0:T(8,128)(2,1)}), bf16[8,640,128]{1,2,0:T(8,128)(2,1)}, u32[]{:S(2)}, u32[]{:S(2)}) async-start(bf16[8,640,128]{1,2,0:T(8,128)(2,1)} %bitcast.67), calls=%async_computation.3 | async-start | bytes 2621440 | tf_op jit(solution)/shard_map/all_to_all | solution.py:57
  228.8 0.2 reduce_sum.36
  229.0 0.8 copy.19
  229.8 1.5 reduce_sum.37
  231.3 0.8 copy.20
  232.1 38.2 %all-to-all-done.2 = bf16[8,640,128]{1,2,0:T(8,128)(2,1)} async-done(((bf16[8,640,128]{1,2,0:T(8,128)(2,1)}), bf16[8,640,128]{1,2,0:T(8,128)(2,1)}, u32[]{:S(2)}, u32[]{:S(2)}) %all-to-all-start.2) | async-done | bytes 1310752 | tf_op jit(solution)/shard_map/all_to_all | solution.py:57
  270.2 2.2 reduce_sum.38
  272.5 219.1 %reduce-scatter.2.cloned.1.call-done = f32[192,80]{0,1:T(8,128)} async-done(((f32[192,5120]{0,1:T(8,128)}), f32[192,80]{0,1:T(8,128)}) %reduce-scatter.2.cloned.1.call-update) | async-done | bytes 61456 | tf_op jit(solution)/shard_map/reduce_scatter | solution.py:49
  491.5 1.5 convert_element_type.66
Async XLA Ops:
  7.2 76.9 %copy-start = (bf16[192,5120]{1,0:T(8,128)(2,1)S(1)}, bf16[192,5120]{1,0:T(8,128)(2,1)}, u32[]{:S(2)}) copy-start(bf16[192,5120]{1,0:T(8,128)(2,1)} %param.8) | copy-start | bytes 5898244
  7.2 75.3 %copy-start.6 = (f32[40,128]{1,0:T(8,128)S(1)}, f32[40,128]{1,0:T(8,128)}, u32[]{:S(2)}) copy-start(f32[40,128]{1,0:T(8,128)} %param.14) | copy-start | bytes 61444
  7.2 40.3 %all-gather.8.cloned.1.call-start = ((), (), s32[]{:S(2)}) async-start(), calls=%async_computation.6 | async-start | bytes 1474560 | tf_op jit(solution)/shard_map/all_gather | solution.py:33
  7.9 74.5 %all-gather.6.cloned.1.call-start = ((), (), s32[]{:S(2)}) async-start(), calls=%async_computation.5 | async-start | bytes 1474560 | tf_op jit(solution)/shard_map/all_gather | solution.py:34
  8.7 109.0 %all-gather.4.cloned.1.call-start = ((), (), s32[]{:S(2)}) async-start(), calls=%async_computation.4 | async-start | bytes 1474560 | tf_op jit(solution)/shard_map/all_gather | solution.py:35
  9.4 482.1 %reduce-scatter.2.cloned.1.call-start = ((), (), s32[]{:S(2)}) async-start(), calls=%async_computation.7 | async-start | bytes 5324800 | tf_op jit(solution)/shard_map/reduce_scatter | solution.py:49
  84.0 1.1 copy-start.1
  117.7 1.5 copy-start.3
  121.4 0.9 copy-start.4
  121.5 1.3 copy-start.2
  126.0 0.8 copy-start.5
  128.5 44.6 %all-to-all-start = ((bf16[8,640,128]{1,2,0:T(8,128)(2,1)}), bf16[8,640,128]{1,2,0:T(8,128)(2,1)S(1)}, u32[]{:S(2)}, u32[]{:S(2)}) async-start(bf16[8,640,128]{1,2,0:T(8,128)(2,1)} %bitcast.69), calls=%async_computation.1 | async-start | bytes 2621440 | tf_op jit(solution)/shard_map/all_to_all | solution.py:57
  173.1 48.3 %all-to-all-start.1 = ((bf16[8,640,128]{1,2,0:T(8,128)(2,1)}), bf16[8,640,128]{1,2,0:T(8,128)(2,1)}, u32[]{:S(2)}, u32[]{:S(2)}) async-start(bf16[8,640,128]{1,2,0:T(8,128)(2,1)} %bitcast.68), calls=%async_computation.2 | async-start | bytes 2621440 | tf_op jit(solution)/shard_map/all_to_all | solution.py:57
  221.4 48.9 %all-to-all-start.2 = ((bf16[8,640,128]{1,2,0:T(8,128)(2,1)}), bf16[8,640,128]{1,2,0:T(8,128)(2,1)}, u32[]{:S(2)}, u32[]{:S(2)}) async-start(bf16[8,640,128]{1,2,0:T(8,128)(2,1)} %bitcast.67), calls=%async_computation.3 | async-start | bytes 2621440 | tf_op jit(solution)/shard_map/all_to_all | solution.py:57
Sparse Core Ops, SparseCore 0:
  10.1 37.2 all-gather.7
  49.6 32.7 all-gather.5
  84.6 33.0 all-gather.3
  126.1 365.3 reduce-scatter.1
where the time goes:
time: 500 us
  waiting for transfers between devices  438 us (88%)
  starting transfers between devices  19.1 us (4%)
  between operations  13.9 us (3%)
  matrix products  10.8 us (2%)
  local copies, waits for them, and re-layouts  9.32 us (2%)
  other arithmetic  8.55 us (2%)
    reduce_scatter x1, waiting for transfers between devices, body(): lax.psum_scatter(token_terms, 'dp', scatter_dimension=1, tiled=True)  219 us
    all_to_all x3, waiting for transfers between devices, body(): lax.all_to_all(shortened(rounded), 'node', split_axis=0, concat_axis=0, t...  114 us
    all_gather x1, waiting for transfers between devices, body(): lax.all_gather(gate_codes, 'node', axis=0, tiled=True)  37.2 us
    all_gather x1, waiting for transfers between devices, body(): lax.all_gather(up_codes, 'node', axis=0, tiled=True)  33.4 us
    all_gather x1, waiting for transfers between devices, body(): lax.all_gather(down_codes, 'node', axis=1, tiled=True)  31.9 us
    all_to_all x3, starting transfers between devices, body(): lax.all_to_all(shortened(rounded), 'node', split_axis=0, concat_axis=0, t...  19 us
  transfers between devices with their start and end apart: 7, of which 7 were waited for; matrix products, arithmetic and copies ran while one was open for 4% of the time, Pallas kernels for 0%

commit v1 on v0

v1 whole, which is shorter than its diff:
```python
import jax
import jax.numpy as jnp
from jax import lax
from jax.experimental import pallas as pl
from jax.experimental.pallas import tpu as pltpu
from jax.sharding import PartitionSpec as P

BF = jnp.bfloat16
F32 = jnp.float32
MESH = pl.DeviceIdType.MESH

ROWS = 192
WIDE = 640
HID = 128
QB = 128
CUT = 48
N_COLS = 80


def dot_nn(a, b):
    return lax.dot_general(a, b, (((1,), (0,)), ((), ())), preferred_element_type=F32)


def dot_nt(a, b):
    return lax.dot_general(a, b, (((1,), (1,)), ((), ())), preferred_element_type=F32)


def dot_tn(a, b):
    return lax.dot_general(a, b, (((0,), (0,)), ((), ())), preferred_element_type=F32)


def kernel(
    tok, cot, gate_codes, up_codes, down_codes, gate_scales, up_scales, down_scales,
    token_grad, gate_grad, up_grad, down_grad,
    acts_in, w_gu, w_down, mine, other, mate_in, summed, terms_in,
    hidden, grad_out, down_out, grad_in, down_in, grad_own, down_own,
    up_buf, dn_buf, up_in, dn_in, last_buf, last_in,
    send_sems, recv_sems,
):
    dp = lax.axis_index("dp")
    node = lax.axis_index("node")
    z, x, low = dp // 8, (dp // 2) % 4, dp % 2
    chip, core = node // 2, node % 2
    par = x % 2
    mate = node + 1 - 2 * core
    pair = dp + 2 - 4 * par

    def at_z(step):
        return lax.rem(z + step + 8, 8) * 8 + x * 2 + low

    def at_chip(step):
        return lax.rem(chip + step + 4, 4)

    counts = {"send": 0, "recv": 0}

    def fresh(kind, number=1):
        first = counts[kind]
        counts[kind] += number
        return first

    sent = []

    def push(src, dst, recv, to_dp, to_node, when=None):
        copy = pltpu.make_async_remote_copy(
            src_ref=src, dst_ref=dst, send_sem=send_sems.at[fresh("send")], recv_sem=recv_sems.at[recv],
            device_id={"dp": to_dp, "node": to_node}, device_id_type=MESH,
        )
        if when is None:
            copy.start()
        else:
            pl.when(when)(copy.start)
        sent.append((copy, when))

    def landed(dst, recv):
        pltpu.make_async_copy(dst, dst, recv_sems.at[recv]).wait()

    barrier = pltpu.get_barrier_semaphore()

    def greet(to_dp, to_node):
        pl.semaphore_signal(barrier, inc=1, device_id={"dp": to_dp, "node": to_node}, device_id_type=MESH)

    for step in range(1, 8):
        greet(dp, lax.rem(node + step, 8))
    greet(at_z(1), node)
    greet(at_z(-1), node)
    greet(pair, node)
    loop_back = jnp.logical_and(z == node, par == core)
    for half in range(2):
        for hi in range(2):
            for lo in range(2):
                src_dp = (2 * chip + half) * 8 + (core + 2 * hi) * 2 + lo
                self_src = jnp.logical_and(src_dp == dp, z == node)
                pl.when(jnp.logical_not(self_src))(lambda a=src_dp: greet(a, z))

    for b in range(WIDE // QB):
        rows = slice(b * QB, (b + 1) * QB)
        line = pl.ds(node * (WIDE // QB) + b, 1)
        w_gu[0, rows, 0:HID] = (gate_codes[rows, :].astype(F32) * gate_scales[line, :]).astype(BF)
        w_gu[0, rows, HID:] = (up_codes[rows, :].astype(F32) * up_scales[line, :]).astype(BF)
        lanes = lax.broadcasted_iota(jnp.int32, down_scales.shape, 1)
        column = jnp.sum(
            jnp.where(lanes == node * (WIDE // QB) + b, down_scales[...], 0.0), axis=1, keepdims=True
        )
        w_down[0, :, rows] = (down_codes[:, rows].astype(F32) * column).astype(BF)

    pl.semaphore_wait(barrier, 18 - loop_back.astype(jnp.int32))

    is_src = core == par
    mine_cols = pl.ds(pl.multiple_of(node * WIDE, 128), WIDE)
    mate_cols = pl.ds(pl.multiple_of(mate * WIDE, 128), WIDE)
    fetch_recv = [fresh("recv") for _ in range(3)]
    own_recv = [fresh("recv") for _ in range(2)]
    own_rows = pl.ds(pl.multiple_of((z % 4) * CUT, 16), CUT)

    fetch_send = [[fresh("send") for _ in range(2)] for _ in range(3)]

    def fetch_copy(arr, a, step, kk):
        to_node = at_chip(step) * 2 + kk
        return pltpu.make_async_remote_copy(
            src_ref=arr.at[own_rows, pl.ds(pl.multiple_of(to_node * WIDE, 128), WIDE)],
            dst_ref=acts_in.at[a, chip, own_rows, :],
            send_sem=send_sems.at[fetch_send[step - 1][kk]], recv_sem=recv_sems.at[fetch_recv[step - 1]],
            device_id={"dp": dp, "node": to_node}, device_id_type=MESH,
        )

    for a, arr in enumerate((tok, cot)):
        @pl.when(jnp.logical_and(is_src, z // 4 == a))
        def _(a=a, arr=arr):
            for step in (2, 1, 3):
                for kk in range(2):
                    fetch_copy(arr, a, step, kk).start()

    w_recv = [fresh("recv") for _ in range(2)]
    push(w_gu.at[0], w_gu.at[1], w_recv[0], pair, node)
    push(w_down.at[0], w_down.at[1], w_recv[1], pair, node)

    own_copies = []
    for a, arr in enumerate((tok, cot)):
        push(arr.at[:, mate_cols], acts_in.at[a, chip], own_recv[a], dp, mate, when=is_src)

        @pl.when(is_src)
        def _(a=a, arr=arr):
            pltpu.make_async_copy(
                arr.at[:, mine_cols], acts_in.at[a, chip], recv_sems.at[own_recv[a]]
            ).start()

    up_recv = [[fresh("recv") for _ in range(3)] for _ in range(3)]
    dn_recv = [[fresh("recv") for _ in range(3)] for _ in range(3)]
    far_recv = [fresh("recv") for _ in range(3)]

    def block(turn, step):
        piece = lax.rem(z + turn + 8, 8)
        return acts_in.at[
            piece // 4, at_chip(-step), pl.ds(pl.multiple_of((piece % 4) * CUT, 16), CUT), :
        ]

    def relay(turn):
        for step in (1, 3, 2):
            if turn == 0:
                landed(block(0, step), fetch_recv[step - 1])
                push(block(0, step), block(0, step), up_recv[0][step - 1], at_z(1), node)
                push(block(0, step), block(0, step), dn_recv[0][step - 1], at_z(-1), node)
                continue
            if turn == 4:
                landed(block(4, step), far_recv[step - 1])
                continue
            here = block(-turn, step)
            landed(here, up_recv[turn - 1][step - 1])
            if turn < 3:
                push(here, here, up_recv[turn][step - 1], at_z(1), node)
            elif step != 3:
                push(here, here, far_recv[step - 1], at_z(1), node, when=None if step == 1 else core == 0)
            here = block(turn, step)
            landed(here, dn_recv[turn - 1][step - 1])
            if turn < 3:
                push(here, here, dn_recv[turn][step - 1], at_z(-1), node)
            elif step != 1:
                push(here, here, far_recv[step - 1], at_z(-1), node, when=None if step == 3 else core == 1)

    mate_recv = [fresh("recv") for _ in range(8)]
    mate_send = [fresh("send") for _ in range(8)]
    term_recv = [[fresh("recv") for _ in range(3)] for _ in range(8)]
    term_send = [[fresh("send") for _ in range(3)] for _ in range(8)]
    spans = (slice(0, 2 * HID), slice(2 * HID, 3 * HID))

    def place(turn):
        piece = lax.rem(z + turn + 8, 8)
        return piece // 4, pl.ds(pl.multiple_of((piece % 4) * CUT, 16), CUT)

    def mate_copy(turn, a, rows):
        return pltpu.make_async_remote_copy(
            src_ref=other.at[:, rows, spans[a]], dst_ref=mate_in.at[:, rows, spans[a]],
            send_sem=send_sems.at[mate_send[turn]], recv_sem=recv_sems.at[mate_recv[turn]],
            device_id={"dp": dp, "node": mate}, device_id_type=MESH,
        )

    def term_copy(turn, a, rows, step):
        return pltpu.make_async_remote_copy(
            src_ref=summed.at[at_chip(step), rows, spans[a]], dst_ref=terms_in.at[step - 1, rows, spans[a]],
            send_sem=send_sems.at[term_send[turn][step - 1]], recv_sem=recv_sems.at[term_recv[turn][step - 1]],
            device_id={"dp": dp, "node": at_chip(step) * 2 + core}, device_id_type=MESH,
        )

    def multiply(turn):
        which, rows = place(turn)
        for a in range(2):
            @pl.when(which == a)
            def _(a=a):
                data = acts_in[a, :, rows, :].reshape(4 * CUT, WIDE)
                for part, store in ((1 - core, other), (core, mine)):
                    if a == 0:
                        out = dot_nn(data, w_gu[part])
                    else:
                        out = dot_nt(data, w_down[part])
                    store[:, rows, spans[a]] = out.reshape(4, CUT, -1).astype(store.dtype)
                    if store is other:
                        mate_copy(turn % 8, a, rows).start()

    def combine(turn):
        which, rows = place(turn)
        for a in range(2):
            @pl.when(which == a)
            def _(a=a):
                mate_copy(turn % 8, a, rows).wait_recv()
                total = mine[:, rows, spans[a]] + mate_in[:, rows, spans[a]].astype(F32)
                mine[:, rows, spans[a]] = total
                summed[:, rows, spans[a]] = total.astype(BF)
                for step in (2, 1, 3):
                    term_copy(turn % 8, a, rows, step).start()

    def collect(turn):
        which, rows = place(turn)
        for a in range(2):
            @pl.when(which == a)
            def _(a=a):
                for step in range(1, 4):
                    term_copy(turn % 8, a, rows, step).wait_recv()

    relay(0)
    for a in range(2):
        landed(acts_in.at[a, chip], own_recv[a])
    relay(1)
    landed(w_gu.at[1], w_recv[0])
    landed(w_down.at[1], w_recv[1])
    multiply(0)
    relay(2)
    multiply(-1)
    combine(0)
    multiply(1)
    combine(-1)
    relay(3)
    multiply(-2)
    combine(1)
    multiply(2)
    combine(-2)
    multiply(-3)
    combine(2)
    multiply(3)
    combine(-3)
    relay(4)
    multiply(4)
    combine(3)
    combine(4)
    for turn in range(8):
        collect(turn)

    full = mine[chip]
    for step in range(3):
        full = full + terms_in[step].astype(F32)
    gate, upper, d_act = full[:, 0:HID], full[:, HID : 2 * HID], full[:, 2 * HID :]
    sig = jax.nn.sigmoid(gate)
    silu = gate * sig
    hidden[core, chip, :, 0:HID] = (d_act * upper * sig * (1.0 + gate * (1.0 - sig))).astype(BF)
    hidden[core, chip, :, HID : 2 * HID] = (d_act * silu).astype(BF)
    hidden[core, chip, :, 2 * HID :] = (silu * upper).astype(BF)

    hid_recv = [fresh("recv") for _ in range(3)]
    hid_mate = [fresh("recv") for _ in range(4)]
    own_hid = hidden.at[core, chip]
    for step in (2, 1, 3):
        push(own_hid, own_hid, hid_recv[step - 1], dp, at_chip(step) * 2 + core)
    push(own_hid, own_hid, hid_mate[0], dp, mate)
    for step in (1, 3, 2):
        here = hidden.at[core, at_chip(-step)]
        landed(here, hid_recv[step - 1])
        push(here, here, hid_mate[step], dp, mate)
    for step in range(4):
        landed(hidden.at[1 - core, at_chip(-step)], hid_mate[step])

    def weight_grads(part):
        tokens = acts_in[0].reshape(4 * ROWS, WIDE)
        grads = acts_in[1].reshape(4 * ROWS, WIDE)
        back = hidden[part].reshape(4 * ROWS, 3 * HID)
        return dot_tn(tokens, back[:, 0 : 2 * HID]), dot_tn(back[:, 2 * HID :], grads)

    first, second = weight_grads(1)
    grad_out[...] = first.astype(BF)
    down_out[...] = second.astype(BF)
    grad_recv = [fresh("recv") for _ in range(2)]
    push(grad_out, grad_in, grad_recv[0], pair, node)
    push(down_out, down_in, grad_recv[1], pair, node)

    def token_terms(turn):
        piece = lax.rem(z + turn + 8, 8)
        rows = pl.ds(pl.multiple_of((piece % 2) * 96, 16), 96)
        return sum(
            dot_nt(hidden[part, piece // 2, rows, 0 : 2 * HID], w_gu[part]) for part in range(2)
        )

    ring = {}
    for way in (1, -1):
        for far in range(1, 5):
            for cut in range(2):
                if far == 4 and cut != (0 if way == 1 else 1):
                    continue
                ring[way, far, cut] = fresh("recv")

    def cut_rows(cut):
        return slice(cut * CUT, (cut + 1) * CUT)

    def ring_step(way, far, terms):
        buf, into = (up_buf, up_in) if way == 1 else (dn_buf, dn_in)
        for cut in range(2):
            if (way, far, cut) not in ring:
                continue
            rows = cut_rows(cut)
            value = terms[rows]
            if (way, far + 1, cut) in ring:
                landed(into.at[far, rows], ring[way, far + 1, cut])
                value = value + into[far, rows].astype(F32)
            buf[far - 1, rows] = value.astype(BF)
            push(buf.at[far - 1, rows], into.at[far - 1, rows], ring[way, far, cut], at_z(way), node)

    terms = token_terms(4)
    ring_step(1, 4, terms)
    ring_step(-1, 4, terms)
    for far in (3, 2, 1):
        ahead = token_terms(far)
        behind = token_terms(-far)
        ring_step(1, far, ahead)
        ring_step(-1, far, behind)
    terms = token_terms(0)

    first, second = weight_grads(0)
    grad_own[...] = first
    down_own[...] = second

    for way, into in ((1, up_in), (-1, dn_in)):
        for cut in range(2):
            landed(into.at[0, cut_rows(cut)], ring[way, 1, cut])
    terms = terms + up_in[0].astype(F32) + dn_in[0].astype(F32)
    for i in range(8):
        last_buf[i, :, 0:N_COLS] = terms[:, i * N_COLS : (i + 1) * N_COLS].astype(BF)
        last_buf[i, :, N_COLS:] = jnp.zeros((96, 128 - N_COLS), BF)

    last_recv = fresh("recv", 8)
    slot = (z % 2) * 4 + (x // 2) * 2 + low
    last_node = 2 * (z // 2) + par
    for i in range(8):
        to_dp = node * 8 + i
        to_self = jnp.logical_and(to_dp == dp, last_node == node)
        push(last_buf.at[i], last_in.at[slot], last_recv + slot, to_dp, last_node, when=jnp.logical_not(to_self))

        @pl.when(to_self)
        def _(i=i):
            pltpu.make_async_copy(last_buf.at[i], last_in.at[slot], recv_sems.at[last_recv + slot]).start()

    landed(grad_in, grad_recv[0])
    landed(down_in, grad_recv[1])
    gate_grad[...] = (grad_own[:, 0:HID] + grad_in[:, 0:HID].astype(F32)).astype(BF)
    up_grad[...] = (grad_own[:, HID:] + grad_in[:, HID:].astype(F32)).astype(BF)
    down_grad[...] = (down_own[...] + down_in[...].astype(F32)).astype(BF)

    for i in range(8):
        landed(last_in.at[i], last_recv + i)
    for half in range(2):
        total = last_in[4 * half].astype(F32)
        for i in range(1, 4):
            total = total + last_in[4 * half + i].astype(F32)
        token_grad[half * 96 : (half + 1) * 96, :] = total[:, 0:N_COLS].astype(BF)

    for copy, when in sent:
        if when is None:
            copy.wait_send()
        else:
            pl.when(when)(copy.wait_send)
    for a, arr in enumerate((tok, cot)):
        @pl.when(jnp.logical_and(is_src, z // 4 == a))
        def _(a=a, arr=arr):
            for step in range(1, 4):
                for kk in range(2):
                    fetch_copy(arr, a, step, kk).wait_send()
    for turn in range(8):
        which, rows = place(turn)
        for a in range(2):
            @pl.when(which == a)
            def _(a=a, turn=turn, rows=rows):
                mate_copy(turn, a, rows).wait_send()
                for step in range(1, 4):
                    term_copy(turn, a, rows, step).wait_send()


def body(*args):
    vmem = pl.BlockSpec(memory_space=pltpu.VMEM)
    hbm = pl.BlockSpec(memory_space=pl.ANY)
    return pl.pallas_call(
        kernel,
        out_shape=(
            jax.ShapeDtypeStruct((ROWS, N_COLS), BF),
            jax.ShapeDtypeStruct((WIDE, HID), BF),
            jax.ShapeDtypeStruct((WIDE, HID), BF),
            jax.ShapeDtypeStruct((HID, WIDE), BF),
        ),
        in_specs=[hbm, hbm] + [vmem] * 6,
        out_specs=(vmem,) * 4,
        scratch_shapes=[
            pltpu.VMEM((2, 4, ROWS, WIDE), BF),
            pltpu.VMEM((2, WIDE, 2 * HID), BF),
            pltpu.VMEM((2, HID, WIDE), BF),
            pltpu.VMEM((4, ROWS, 3 * HID), F32),
            pltpu.VMEM((4, ROWS, 3 * HID), BF),
            pltpu.VMEM((4, ROWS, 3 * HID), BF),
            pltpu.VMEM((4, ROWS, 3 * HID), BF),
            pltpu.VMEM((3, ROWS, 3 * HID), BF),
            pltpu.VMEM((2, 4, ROWS, 3 * HID), BF),
            pltpu.VMEM((WIDE, 2 * HID), BF),
            pltpu.VMEM((HID, WIDE), BF),
            pltpu.VMEM((WIDE, 2 * HID), BF),
            pltpu.VMEM((HID, WIDE), BF),
            pltpu.VMEM((WIDE, 2 * HID), F32),
            pltpu.VMEM((HID, WIDE), F32),
            pltpu.VMEM((4, 96, WIDE), BF),
            pltpu.VMEM((4, 96, WIDE), BF),
            pltpu.VMEM((4, 96, WIDE), BF),
            pltpu.VMEM((4, 96, WIDE), BF),
            pltpu.VMEM((8, 96, 128), BF),
            pltpu.VMEM((8, 96, 128), BF),
            pltpu.SemaphoreType.DMA((112,)),
            pltpu.SemaphoreType.DMA((112,)),
        ],
        compiler_params=pltpu.CompilerParams(
            collective_id=0, has_side_effects=True, vmem_limit_bytes=48 * 1024 * 1024
        ),
        cost_estimate=pl.CostEstimate(flops=2_100_000_000, bytes_accessed=5_000_000, transcendentals=25_000),
    )(*args)


def solution(mesh):
    return jax.shard_map(
        body,
        mesh=mesh,
        in_specs=(
            P("node", None),
            P("node", None),
            P("node", "dp"),
            P("node", "dp"),
            P("dp", "node"),
            P(None, "dp"),
            P(None, "dp"),
            P("dp", None),
        ),
        out_specs=(P("node", "dp"), P("node", "dp"), P("node", "dp"), P("dp", "node")),
        check_vma=False,
    )
```

time: 500 us -> 114 us (0.23)
  the two profiles are of different devices: /device:TPU:16 before, /device:TPU:62 now
where the time goes in v1:
time: 114 us
  Pallas kernels  102 us (89%)
  local copies, waits for them, and re-layouts  10.8 us (9%)
    pallas_call x1, Pallas kernels, body(): pl.pallas_call(kernel, out_shape=(jax.ShapeDtypeStruct((ROWS, N_COLS), BF...  102 us
    unnamed x18, local copies, waits for them, and re-layouts  10.1 us

profile of v1, /device:TPU:62, one launch (start us, length us, event | category | flops | bytes accessed | tf_op | source)
XLA Modules:
  0.0 113.6 jit_solution(4506657188170268883)
XLA Ops:
  0.6 0.8 copy.12.down_scales
  1.5 0.0 copy-start
  1.5 1.5 %copy-done = bf16[192,5120]{1,0:T(8,128)(2,1)S(1)} copy-done((bf16[192,5120]{1,0:T(8,128)(2,1)S(1)}, bf16[192,5120]{1,0:T(8,128)(2,1)}, u32[]{:S(2)}) %copy-start) | copy-done | bytes 1966104
  3.0 0.0 copy-start.1
  3.0 1.5 %copy-done.1 = bf16[192,5120]{1,0:T(8,128)(2,1)S(1)} copy-done((bf16[192,5120]{1,0:T(8,128)(2,1)S(1)}, bf16[192,5120]{1,0:T(8,128)(2,1)}, u32[]{:S(2)}) %copy-start.1) | copy-done | bytes 1966104
  4.6 0.0 copy-start.2
  4.6 0.9 copy-done.2
  5.5 0.0 copy-start.3
  5.5 0.9 copy-done.3
  6.4 0.0 copy-start.4
  6.4 0.9 copy-done.4
  7.3 0.0 copy-start.5
  7.3 0.7 copy-done.5
  8.0 0.0 copy-start.6
  8.0 0.7 copy-done.6
  8.8 102.2 %shard_map.111 = (bf16[192,80]{1,0:T(8,128)(2,1)S(1)}, bf16[640,128]{1,0:T(8,128)(2,1)S(1)}, bf16[640,128]{1,0:T(8,128)(2,1)S(1)}, bf16[128,640]{1,0:T(8,128)(2,1)S(1)}) custom-call(bf16[192,5120]{1,0:T(8,128)(2,1)S(1)} %copy-done, bf16[192,5120]{1,0:T(8,128)(2,1)S(1)} %copy-done.1, bf16[640,128]{1,0:T(8,128)(2,1)S(1)} %copy-done.2, ...), custom_call_target="tpu_custom_call" | custom-call | flops 2100000000 | bytes 5000000 | tf_op jit(solution)/shard_map/pallas_call | solution.py:406
  110.9 0.7 copy.13
  111.6 0.7 copy.17
  112.3 0.7 copy.18
  113.0 0.7 copy.19
Async XLA Ops:
  1.5 1.6 %copy-start = (bf16[192,5120]{1,0:T(8,128)(2,1)S(1)}, bf16[192,5120]{1,0:T(8,128)(2,1)}, u32[]{:S(2)}) copy-start(bf16[192,5120]{1,0:T(8,128)(2,1)} %tok.1) | copy-start | bytes 5898244
  3.0 1.5 %copy-start.1 = (bf16[192,5120]{1,0:T(8,128)(2,1)S(1)}, bf16[192,5120]{1,0:T(8,128)(2,1)}, u32[]{:S(2)}) copy-start(bf16[192,5120]{1,0:T(8,128)(2,1)} %cot.1) | copy-start | bytes 5898244
  4.6 0.9 copy-start.2
  5.5 0.9 copy-start.3
  6.4 0.9 copy-start.4
  7.3 0.7 copy-start.5
  8.0 0.7 copy-start.6

commit v2 on v1

v2 whole, which is shorter than its diff:
```python
import jax
import jax.numpy as jnp
from jax import lax
from jax.experimental import pallas as pl
from jax.experimental.pallas import tpu as pltpu
from jax.sharding import PartitionSpec as P

BF = jnp.bfloat16
F32 = jnp.float32
MESH = pl.DeviceIdType.MESH

ROWS = 192
WIDE = 640
HID = 128
QB = 128
CUT = 48
VMEM_BYTES = 60 * 1024 * 1024
N_COLS = 80


def dot_nn(a, b):
    return lax.dot_general(a, b, (((1,), (0,)), ((), ())), preferred_element_type=F32)


def dot_nt(a, b):
    return lax.dot_general(a, b, (((1,), (1,)), ((), ())), preferred_element_type=F32)


def dot_tn(a, b):
    return lax.dot_general(a, b, (((0,), (0,)), ((), ())), preferred_element_type=F32)


def kernel(
    tok, cot, gate_codes_hbm, up_codes_hbm, down_codes_hbm, gate_scales_hbm, up_scales_hbm, down_scales_hbm,
    token_grad_hbm, gate_grad_hbm, up_grad_hbm, down_grad_hbm,
    token_grad, gate_grad, up_grad, down_grad, gate_codes, up_codes, down_codes, gate_scales, up_scales, down_scales,
    acts_in, fetch_relay, w_gu, w_down, mine, other, mate_in, far_out, far_in, near_out, near_in,
    hidden, grad_out, down_out, grad_in, down_in, grad_own, down_own,
    up_buf, dn_buf, up_in, dn_in, side_buf, side_in, last_buf, last_in,
    load_sems, store_sems, send_sems, recv_sems,
):
    dp = lax.axis_index("dp")
    node = lax.axis_index("node")
    z, x, low = dp // 8, (dp // 2) % 4, dp % 2
    chip, core = node // 2, node % 2
    par = x % 2
    mate = node + 1 - 2 * core
    pair = dp + 2 - 4 * par
    toward = 1 - 2 * core
    side = (x // 2) * 2 + low

    def at_z(step):
        return lax.rem(z + step + 8, 8) * 8 + x * 2 + low

    def at_chip(step):
        return lax.rem(chip + step + 4, 4)

    def at_side(member):
        return z * 8 + (par + 2 * (member // 2)) * 2 + member % 2

    loads = [
        pltpu.make_async_copy(src, dst, load_sems.at[i])
        for i, (src, dst) in enumerate((
            (gate_codes_hbm, gate_codes), (up_codes_hbm, up_codes), (down_codes_hbm, down_codes),
            (gate_scales_hbm, gate_scales), (up_scales_hbm, up_scales), (down_scales_hbm, down_scales),
        ))
    ]
    for load in loads:
        load.start()

    counts = {"send": 0, "recv": 0}

    def fresh(kind, number=1):
        first = counts[kind]
        counts[kind] += number
        return first

    sent = []

    def push(src, dst, recv, to_dp, to_node, when=None):
        copy = pltpu.make_async_remote_copy(
            src_ref=src, dst_ref=dst, send_sem=send_sems.at[fresh("send")], recv_sem=recv_sems.at[recv],
            device_id={"dp": to_dp, "node": to_node}, device_id_type=MESH,
        )
        if when is None:
            copy.start()
        else:
            pl.when(when)(copy.start)
        sent.append((copy, when))

    def landed(dst, recv):
        pltpu.make_async_copy(dst, dst, recv_sems.at[recv]).wait()

    barrier = pltpu.get_barrier_semaphore()

    def greet(to_dp, to_node):
        pl.semaphore_signal(barrier, inc=1, device_id={"dp": to_dp, "node": to_node}, device_id_type=MESH)

    for step in range(1, 8):
        greet(dp, lax.rem(node + step, 8))
    greet(at_z(1), node)
    greet(at_z(-1), node)
    greet(pair, node)
    for step in range(1, 4):
        greet(at_side(lax.rem(side + step, 4)), node)
    loop_back = jnp.logical_and(jnp.logical_and(z == node, par == core), low == par)
    for half in range(2):
        src_dp = (2 * chip + half) * 8 + (core + 2 * (x // 2)) * 2 + par
        self_src = jnp.logical_and(src_dp == dp, z == node)
        pl.when(jnp.logical_not(self_src))(lambda a=src_dp: greet(a, z))

    for load in loads:
        load.wait()
    eye = lax.broadcasted_iota(jnp.int32, (HID, HID), 0) == lax.broadcasted_iota(jnp.int32, (HID, HID), 1)
    for b in range(WIDE // QB):
        rows = slice(b * QB, (b + 1) * QB)
        line = pl.ds(node * (WIDE // QB) + b, 1)
        w_gu[0, rows, 0:HID] = (gate_codes[rows, :].astype(F32) * gate_scales[line, :]).astype(BF)
        w_gu[0, rows, HID:] = (up_codes[rows, :].astype(F32) * up_scales[line, :]).astype(BF)
        column = jnp.sum(jnp.where(eye, down_scales[line, :], 0.0), axis=1, keepdims=True)
        w_down[0, :, rows] = (down_codes[:, rows].astype(F32) * column).astype(BF)

    pl.semaphore_wait(barrier, 15 - loop_back.astype(jnp.int32))

    def quarter_rows(quarter):
        return pl.ds(pl.multiple_of(quarter * CUT, 16), CUT)

    def cols_of(to_node):
        return pl.ds(pl.multiple_of(to_node * WIDE, 128), WIDE)

    is_src = core == par
    fetch_recv = [fresh("recv") for _ in range(3)]
    relay_recv = fresh("recv")
    own_recv = [fresh("recv") for _ in range(2)]
    fetch_send = [[fresh("send") for _ in range(2)] for _ in range(3)]
    own_rows = quarter_rows(z // 2)

    def fetch_copy(arr, a, step, kk):
        owner = at_chip(step) * 2 + kk
        if step == 2:
            dst, to_node, recv = fetch_relay, at_chip(1 - 2 * kk) * 2 + kk, relay_recv
        else:
            dst, to_node, recv = acts_in.at[a, chip, own_rows, :], owner, fetch_recv[step - 1]
        return pltpu.make_async_remote_copy(
            src_ref=arr.at[own_rows, cols_of(owner)], dst_ref=dst,
            send_sem=send_sems.at[fetch_send[step - 1][kk]], recv_sem=recv_sems.at[recv],
            device_id={"dp": dp, "node": to_node}, device_id_type=MESH,
        )

    for a, arr in enumerate((tok, cot)):
        @pl.when(jnp.logical_and(is_src, z % 2 == a))
        def _(a=a, arr=arr):
            for step in (2, 1, 3):
                for kk in range(2):
                    fetch_copy(arr, a, step, kk).start()

    w_recv = [fresh("recv") for _ in range(2)]
    push(w_gu.at[0], w_gu.at[1], w_recv[0], pair, node)
    push(w_down.at[0], w_down.at[1], w_recv[1], pair, node)

    for a, arr in enumerate((tok, cot)):
        push(arr.at[:, cols_of(mate)], acts_in.at[a, chip], own_recv[a], dp, mate, when=is_src)

        @pl.when(is_src)
        def _(a=a, arr=arr):
            pltpu.make_async_copy(
                arr.at[:, cols_of(node)], acts_in.at[a, chip], recv_sems.at[own_recv[a]]
            ).start()

    up_recv = [[fresh("recv") for _ in range(3)] for _ in range(3)]
    dn_recv = [[fresh("recv") for _ in range(3)] for _ in range(3)]
    far_recv = [fresh("recv") for _ in range(3)]

    def block(turn, step):
        piece = lax.rem(z + turn + 8, 8)
        return acts_in.at[piece % 2, at_chip(-step), quarter_rows(piece // 2), :]

    def relay(turn, step):
        if turn == 0:
            landed(block(0, step), fetch_recv[step - 1])
            push(block(0, step), block(0, step), up_recv[0][step - 1], at_z(1), node)
            push(block(0, step), block(0, step), dn_recv[0][step - 1], at_z(-1), node)
            return
        if turn == 4:
            landed(block(4, step), far_recv[step - 1])
            return
        here = block(-turn, step)
        landed(here, up_recv[turn - 1][step - 1])
        if turn < 3:
            push(here, here, up_recv[turn][step - 1], at_z(1), node)
        elif step != 3:
            push(here, here, far_recv[step - 1], at_z(1), node, when=None if step == 1 else core == 0)
        here = block(turn, step)
        landed(here, dn_recv[turn - 1][step - 1])
        if turn < 3:
            push(here, here, dn_recv[turn][step - 1], at_z(-1), node)
        elif step != 1:
            push(here, here, far_recv[step - 1], at_z(-1), node, when=None if step == 3 else core == 1)

    sign = 1 - 2 * (z % 2)
    quarters = [
        lax.rem(z + first * sign + 8, 8) // 2 for first in (0, -1, 2, -3)
    ]
    mate_recv = [fresh("recv") for _ in range(4)]
    relay_sum_recv = [[fresh("recv") for _ in range(3)] for _ in range(4)]
    near_recv = [[fresh("recv") for _ in range(2)] for _ in range(4)]
    hid_near = [[fresh("recv") for _ in range(2)] for _ in range(4)]
    hid_far = [[fresh("recv") for _ in range(3)] for _ in range(4)]
    hid_mate = [[fresh("recv") for _ in range(4)] for _ in range(4)]
    near_steps = (1, -1)
    ways = (1, toward, -1)
    lane = lax.broadcasted_iota(jnp.int32, (CUT, 3 * HID), 1)
    goes_up = lane < 2 * HID - core * HID

    def cols(b):
        return slice(b * HID, (b + 1) * HID)

    def multiply(s):
        rows = quarter_rows(quarters[s])
        tokens = acts_in[0, :, rows, :].reshape(4 * CUT, WIDE)
        grads = acts_in[1, :, rows, :].reshape(4 * CUT, WIDE)
        for part, store in ((1 - core, other), (core, mine)):
            store[s, :, :, 0 : 2 * HID] = (
                dot_nn(tokens, w_gu[part]).reshape(4, CUT, 2 * HID).astype(store.dtype)
            )
            store[s, :, :, 2 * HID :] = (
                dot_nt(grads, w_down[part]).reshape(4, CUT, HID).astype(store.dtype)
            )
            if store is other:
                push(other.at[s], mate_in.at[s], mate_recv[s], dp, mate)

    def combine(s):
        landed(mate_in.at[s], mate_recv[s])
        opposite = at_chip(2)
        far_out[s] = (mine[s, opposite] + mate_in[s, opposite].astype(F32)).astype(BF)
        for b in range(3):
            push(
                far_out.at[s, :, cols(b)], far_in.at[s, :, cols(b)], relay_sum_recv[s][b],
                dp, at_chip(ways[b]) * 2 + core,
            )

    def forward_sum(s):
        for b in range(3):
            landed(far_in.at[s, :, cols(b)], relay_sum_recv[s][b])
        passing = far_in[s].astype(F32)
        for i, step in enumerate(near_steps):
            to = at_chip(step)
            extra = jnp.where(goes_up, passing, 0.0) if step == 1 else jnp.where(goes_up, 0.0, passing)
            near_out[s, i] = (mine[s, to] + mate_in[s, to].astype(F32) + extra).astype(BF)
            push(near_out.at[s, i], near_in.at[s, i], near_recv[s][i], dp, to * 2 + core)

    def activate(s):
        full = mine[s, chip] + mate_in[s, chip].astype(F32)
        for i in range(2):
            landed(near_in.at[s, i], near_recv[s][i])
            full = full + near_in[s, i].astype(F32)
        rows = quarter_rows(quarters[s])
        gate, upper, d_act = full[:, 0:HID], full[:, HID : 2 * HID], full[:, 2 * HID :]
        sig = jax.nn.sigmoid(gate)
        silu = gate * sig
        hidden[core, chip, rows, 0:HID] = (d_act * upper * sig * (1.0 + gate * (1.0 - sig))).astype(BF)
        hidden[core, chip, rows, HID : 2 * HID] = (d_act * silu).astype(BF)
        hidden[core, chip, rows, 2 * HID :] = (silu * upper).astype(BF)
        own = hidden.at[core, chip, rows]
        for i, step in enumerate(near_steps):
            push(own, own, hid_near[s][i], dp, at_chip(step) * 2 + core)
        push(own, own, hid_mate[s][0], dp, mate)

    def forward_hidden(s):
        rows = quarter_rows(quarters[s])
        for i, step in enumerate(near_steps):
            landed(hidden.at[core, at_chip(-step), rows], hid_near[s][i])
        for b in range(3):
            here = hidden.at[core, at_chip(-ways[b]), rows, cols(b)]
            push(here, here, hid_far[s][b], dp, at_chip(ways[b]) * 2 + core)
        for i, step in enumerate(near_steps):
            here = hidden.at[core, at_chip(-step), rows]
            push(here, here, hid_mate[s][1 + i], dp, mate)

    def last_hidden(s):
        rows = quarter_rows(quarters[s])
        for b in range(3):
            landed(hidden.at[core, at_chip(2), rows, cols(b)], hid_far[s][b])
        here = hidden.at[core, at_chip(2), rows]
        push(here, here, hid_mate[s][3], dp, mate)

    def finish_hidden(s):
        rows = quarter_rows(quarters[s])
        for i, step in enumerate((0, -1, 1, 2)):
            landed(hidden.at[1 - core, at_chip(step), rows], hid_mate[s][i])

    landed(fetch_relay, relay_recv)
    passed = acts_in.at[z % 2, at_chip(-toward), own_rows, :]
    push(fetch_relay, passed, fetch_recv[1], dp, at_chip(toward) * 2 + core)
    relay(0, 1)
    relay(0, 3)
    relay(0, 2)
    relay(1, 1)
    relay(1, 3)
    for a in range(2):
        landed(acts_in.at[a, chip], own_recv[a])
    relay(1, 2)
    landed(w_gu.at[1], w_recv[0])
    landed(w_down.at[1], w_recv[1])
    multiply(0)
    relay(2, 1)
    combine(0)
    relay(2, 3)
    relay(2, 2)
    multiply(1)
    forward_sum(0)
    relay(3, 1)
    combine(1)
    activate(0)
    relay(3, 3)
    relay(3, 2)
    multiply(2)
    forward_sum(1)
    forward_hidden(0)
    relay(4, 1)
    combine(2)
    activate(1)
    relay(4, 3)
    relay(4, 2)
    multiply(3)
    forward_sum(2)
    last_hidden(0)
    forward_hidden(1)
    combine(3)
    activate(2)
    last_hidden(1)
    forward_sum(3)
    forward_hidden(2)
    activate(3)
    last_hidden(2)
    forward_hidden(3)
    last_hidden(3)
    for s in range(4):
        finish_hidden(s)

    def token_terms(turn):
        piece = lax.rem(z + turn + 8, 8)
        rows = pl.ds(pl.multiple_of((piece % 2) * 96, 16), 96)
        return sum(
            dot_nt(hidden[part, piece // 2, rows, 0 : 2 * HID], w_gu[part]) for part in range(2)
        )

    ring = {}
    for way in (1, -1):
        for far in range(1, 5):
            for cut in range(2):
                if far == 4 and cut != (0 if way == 1 else 1):
                    continue
                ring[way, far, cut] = fresh("recv")

    def cut_rows(cut):
        return slice(cut * CUT, (cut + 1) * CUT)

    def ring_step(way, far, terms):
        buf, into = (up_buf, up_in) if way == 1 else (dn_buf, dn_in)
        for cut in range(2):
            if (way, far, cut) not in ring:
                continue
            rows = cut_rows(cut)
            value = terms[rows]
            if (way, far + 1, cut) in ring:
                landed(into.at[far, rows], ring[way, far + 1, cut])
                value = value + into[far, rows].astype(F32)
            buf[far - 1, rows] = value.astype(BF)
            push(buf.at[far - 1, rows], into.at[far - 1, rows], ring[way, far, cut], at_z(way), node)

    def weight_grads(part):
        tokens = acts_in[0].reshape(4 * ROWS, WIDE)
        grads = acts_in[1].reshape(4 * ROWS, WIDE)
        back = hidden[part].reshape(4 * ROWS, 3 * HID)
        return dot_tn(tokens, back[:, 0 : 2 * HID]), dot_tn(back[:, 2 * HID :], grads)

    terms = token_terms(4)
    ring_step(1, 4, terms)
    ring_step(-1, 4, terms)

    first, second = weight_grads(1)
    grad_out[...] = first.astype(BF)
    down_out[...] = second.astype(BF)
    grad_recv = [fresh("recv") for _ in range(2)]
    push(grad_out, grad_in, grad_recv[0], pair, node)
    push(down_out, down_in, grad_recv[1], pair, node)

    for far in (3, 2, 1):
        ahead = token_terms(far)
        behind = token_terms(-far)
        ring_step(1, far, ahead)
        ring_step(-1, far, behind)
    terms = token_terms(0)

    first, second = weight_grads(0)
    grad_own[...] = first
    down_own[...] = second

    for way, into in ((1, up_in), (-1, dn_in)):
        for cut in range(2):
            landed(into.at[0, cut_rows(cut)], ring[way, 1, cut])
    terms = terms + up_in[0].astype(F32) + dn_in[0].astype(F32)
    for i in range(8):
        side_buf[i // 2, i % 2, :, 0:N_COLS] = terms[:, i * N_COLS : (i + 1) * N_COLS].astype(BF)
        side_buf[i // 2, i % 2, :, N_COLS:] = jnp.zeros((96, 128 - N_COLS), BF)

    side_recv = [fresh("recv") for _ in range(3)]
    for step in range(1, 4):
        to = lax.rem(side + step, 4)
        push(side_buf.at[to], side_in.at[step - 1], side_recv[step - 1], at_side(to), node)
    total = side_buf[side].astype(F32)
    for step in range(1, 4):
        landed(side_in.at[step - 1], side_recv[step - 1])
        total = total + side_in[step - 1].astype(F32)
    last_buf[...] = total.astype(BF)

    last_recv = fresh("recv", 2)
    slot = z % 2
    last_node = 2 * (z // 2) + par
    for i in range(2):
        to_dp = node * 8 + side * 2 + i
        to_self = jnp.logical_and(to_dp == dp, last_node == node)
        push(last_buf.at[i], last_in.at[slot], last_recv + slot, to_dp, last_node, when=jnp.logical_not(to_self))

        @pl.when(to_self)
        def _(i=i):
            pltpu.make_async_copy(last_buf.at[i], last_in.at[slot], recv_sems.at[last_recv + slot]).start()

    landed(grad_in, grad_recv[0])
    landed(down_in, grad_recv[1])
    gate_grad[...] = (grad_own[:, 0:HID] + grad_in[:, 0:HID].astype(F32)).astype(BF)
    up_grad[...] = (grad_own[:, HID:] + grad_in[:, HID:].astype(F32)).astype(BF)
    down_grad[...] = (down_own[...] + down_in[...].astype(F32)).astype(BF)
    stores = [
        pltpu.make_async_copy(src, dst, store_sems.at[i])
        for i, (src, dst) in enumerate((
            (gate_grad, gate_grad_hbm), (up_grad, up_grad_hbm), (down_grad, down_grad_hbm),
            (token_grad, token_grad_hbm),
        ))
    ]
    for store in stores[:3]:
        store.start()

    for i in range(2):
        landed(last_in.at[i], last_recv + i)
    token_grad[...] = jnp.transpose(last_in[...].reshape(ROWS, 128).astype(F32))[0:N_COLS, :].astype(BF)
    stores[3].start()

    for copy, when in sent:
        if when is None:
            copy.wait_send()
        else:
            pl.when(when)(copy.wait_send)
    for a, arr in enumerate((tok, cot)):
        @pl.when(jnp.logical_and(is_src, z % 2 == a))
        def _(a=a, arr=arr):
            for step in range(1, 4):
                for kk in range(2):
                    fetch_copy(arr, a, step, kk).wait_send()
    for store in stores:
        store.wait()


def write_out(*refs):
    copies = [
        pltpu.make_async_copy(refs[i], refs[4 + i], refs[8].at[i]) for i in range(4)
    ]
    for copy in copies:
        copy.start()
    for copy in copies:
        copy.wait()


def body(tok, cot, gate_codes, up_codes, down_codes, gate_scales, up_scales, down_scales):
    hbm = pl.BlockSpec(memory_space=pltpu.HBM)
    outs = (
        jax.ShapeDtypeStruct((N_COLS, ROWS), BF),
        jax.ShapeDtypeStruct((WIDE, HID), BF),
        jax.ShapeDtypeStruct((WIDE, HID), BF),
        jax.ShapeDtypeStruct((HID, WIDE), BF),
    )
    results = pl.pallas_call(
        kernel,
        out_shape=outs,
        in_specs=[hbm] * 8,
        out_specs=(hbm,) * 4,
        scratch_shapes=[
            pltpu.VMEM((N_COLS, ROWS), BF),
            pltpu.VMEM((WIDE, HID), BF),
            pltpu.VMEM((WIDE, HID), BF),
            pltpu.VMEM((HID, WIDE), BF),
            pltpu.VMEM((WIDE, HID), BF),
            pltpu.VMEM((WIDE, HID), BF),
            pltpu.VMEM((HID, WIDE), BF),
            pltpu.VMEM((40, HID), F32),
            pltpu.VMEM((40, HID), F32),
            pltpu.VMEM((40, HID), F32),
            pltpu.VMEM((2, 4, ROWS, WIDE), BF),
            pltpu.VMEM((CUT, WIDE), BF),
            pltpu.VMEM((2, WIDE, 2 * HID), BF),
            pltpu.VMEM((2, HID, WIDE), BF),
            pltpu.VMEM((4, 4, CUT, 3 * HID), F32),
            pltpu.VMEM((4, 4, CUT, 3 * HID), BF),
            pltpu.VMEM((4, 4, CUT, 3 * HID), BF),
            pltpu.VMEM((4, CUT, 3 * HID), BF),
            pltpu.VMEM((4, CUT, 3 * HID), BF),
            pltpu.VMEM((4, 2, CUT, 3 * HID), BF),
            pltpu.VMEM((4, 2, CUT, 3 * HID), BF),
            pltpu.VMEM((2, 4, ROWS, 3 * HID), BF),
            pltpu.VMEM((WIDE, 2 * HID), BF),
            pltpu.VMEM((HID, WIDE), BF),
            pltpu.VMEM((WIDE, 2 * HID), BF),
            pltpu.VMEM((HID, WIDE), BF),
            pltpu.VMEM((WIDE, 2 * HID), F32),
            pltpu.VMEM((HID, WIDE), F32),
            pltpu.VMEM((4, 96, WIDE), BF),
            pltpu.VMEM((4, 96, WIDE), BF),
            pltpu.VMEM((4, 96, WIDE), BF),
            pltpu.VMEM((4, 96, WIDE), BF),
            pltpu.VMEM((4, 2, 96, 128), BF),
            pltpu.VMEM((3, 2, 96, 128), BF),
            pltpu.VMEM((2, 96, 128), BF),
            pltpu.VMEM((2, 96, 128), BF),
            pltpu.SemaphoreType.DMA((6,)),
            pltpu.SemaphoreType.DMA((4,)),
            pltpu.SemaphoreType.DMA((136,)),
            pltpu.SemaphoreType.DMA((136,)),
        ],
        compiler_params=pltpu.CompilerParams(
            collective_id=0, has_side_effects=True, vmem_limit_bytes=VMEM_BYTES
        ),
        cost_estimate=pl.CostEstimate(flops=2_100_000_000, bytes_accessed=5_000_000, transcendentals=25_000),
    )(tok, cot, gate_codes, up_codes, down_codes, gate_scales, up_scales, down_scales.T)
    results = pl.pallas_call(
        write_out,
        out_shape=outs,
        in_specs=[hbm] * 4,
        out_specs=(hbm,) * 4,
        scratch_shapes=[pltpu.SemaphoreType.DMA((4,))],
        compiler_params=pltpu.CompilerParams(vmem_limit_bytes=VMEM_BYTES),
    )(*results)
    return (results[0].T,) + tuple(results[1:])


def solution(mesh):
    return jax.shard_map(
        body,
        mesh=mesh,
        in_specs=(
            P("node", None),
            P("node", None),
            P("node", "dp"),
            P("node", "dp"),
            P("dp", "node"),
            P(None, "dp"),
            P(None, "dp"),
            P("dp", None),
        ),
        out_specs=(P("node", "dp"), P("node", "dp"), P("node", "dp"), P("dp", "node")),
        check_vma=False,
    )
```

time: 114 us -> 117 us (1.026)
  the two profiles are of different devices: /device:TPU:62 before, /device:TPU:42 now
where the time goes in v2:
time: 117 us
  Pallas kernels  116 us (99%)
    pallas_call x1, Pallas kernels, body(): pl.pallas_call(kernel, out_shape=outs, in_specs=[hbm] * 8, out_specs=(hbm...  98.7 us
    pallas_call x1, Pallas kernels, body(): pl.pallas_call(write_out, out_shape=outs, in_specs=[hbm] * 4, out_specs=(...  17.3 us

profile of v2, /device:TPU:42, one launch (start us, length us, event | category | flops | bytes accessed | tf_op | source)
XLA Modules:
  0.0 116.7 jit_solution(2605598901976039898)
XLA Ops:
  0.6 98.7 %shard_map.111 = (bf16[80,192]{1,0:T(8,128)(2,1)}, bf16[640,128]{1,0:T(8,128)(2,1)}, bf16[640,128]{1,0:T(8,128)(2,1)}, bf16[128,640]{1,0:T(8,128)(2,1)}) custom-call(bf16[192,5120]{1,0:T(8,128)(2,1)} %tok.1, bf16[192,5120]{1,0:T(8,128)(2,1)} %cot.1, bf16[640,128]{1,0:T(8,128)(2,1)} %gate_codes_hbm.1, bf16[640,128]{1,0:T(8,128)(2,1)} %up_codes_hbm.1, ...), custom_call_target="tpu_custom_call" | custom-call | flops 2100000000 | bytes 5000000 | tf_op jit(solution)/shard_map/pallas_call | solution.py:483
  99.4 17.3 %shard_map.112 = (bf16[80,192]{1,0:T(8,128)(2,1)}, bf16[640,128]{1,0:T(8,128)(2,1)}, bf16[640,128]{1,0:T(8,128)(2,1)}, bf16[128,640]{1,0:T(8,128)(2,1)}) custom-call(bf16[80,192]{1,0:T(8,128)(2,1)} %get-tuple-element.12.refs_0_, bf16[640,128]{1,0:T(8,128)(2,1)} %get-tuple-element.13.refs_1_, bf16[640,128]{1,0:T(8,128)(2,1)} %get-tuple-element.14.refs_2_, ...), custom_call_target="tpu_custom_call" | custom-call | tf_op jit(solution)/shard_map/pallas_call | solution.py:535

commit v3 on v2

v3 whole, which is shorter than its diff:
```python
import jax
import jax.numpy as jnp
from jax import lax
from jax.experimental import pallas as pl
from jax.experimental.pallas import tpu as pltpu
from jax.sharding import PartitionSpec as P

BF = jnp.bfloat16
F32 = jnp.float32
MESH = pl.DeviceIdType.MESH

ROWS = 192
WIDE = 640
HID = 128
QB = 128
CUT = 48
VMEM_BYTES = 60 * 1024 * 1024
SEMS = 144
N_COLS = 80


def dot_nn(a, b):
    return lax.dot_general(a, b, (((1,), (0,)), ((), ())), preferred_element_type=F32)


def dot_nt(a, b):
    return lax.dot_general(a, b, (((1,), (1,)), ((), ())), preferred_element_type=F32)


def dot_tn(a, b):
    return lax.dot_general(a, b, (((0,), (0,)), ((), ())), preferred_element_type=F32)


def kernel(
    tok, cot, gate_codes_hbm, up_codes_hbm, down_codes_hbm, gate_scales_hbm, up_scales_hbm, down_scales_hbm,
    token_grad_hbm, gate_grad_hbm, up_grad_hbm, down_grad_hbm,
    token_grad, gate_grad, up_grad, down_grad, gate_codes, up_codes, down_codes, gate_scales, up_scales, down_scales,
    acts_in, fetch_buf, w_gu, w_down, mine, other, mate_in, sum_out, sum_in,
    hidden, grad_out, down_out, grad_in, down_in, grad_own, down_own,
    ring_buf, ring_in, side_buf, side_in, last_buf, last_in,
    load_sems, store_sems, send_sems, recv_sems,
):
    dp = lax.axis_index("dp")
    node = lax.axis_index("node")
    z, x, low = dp // 8, (dp // 2) % 4, dp % 2
    chip, core = node // 2, node % 2
    par = x % 2
    mate = node + 1 - 2 * core
    pair = dp + 2 - 4 * par
    side = (x // 2) * 2 + low

    def at_z(step):
        return lax.rem(z + step + 8, 8) * 8 + x * 2 + low

    def at_chip(step):
        return lax.rem(chip + step + 4, 4)

    def at_side(member):
        return z * 8 + (par + 2 * (member // 2)) * 2 + member % 2

    loads = [
        pltpu.make_async_copy(src, dst, load_sems.at[i])
        for i, (src, dst) in enumerate((
            (gate_codes_hbm, gate_codes), (up_codes_hbm, up_codes), (down_codes_hbm, down_codes),
            (gate_scales_hbm, gate_scales), (up_scales_hbm, up_scales), (down_scales_hbm, down_scales),
        ))
    ]
    for load in loads:
        load.start()

    counts = {"send": 0, "recv": 0}

    def fresh(kind, number=1):
        first = counts[kind]
        counts[kind] += number
        return first

    sent = []

    def push(src, dst, recv, to_dp, to_node, when=None):
        copy = pltpu.make_async_remote_copy(
            src_ref=src, dst_ref=dst, send_sem=send_sems.at[fresh("send")], recv_sem=recv_sems.at[recv],
            device_id={"dp": to_dp, "node": to_node}, device_id_type=MESH,
        )
        if when is None:
            copy.start()
        else:
            pl.when(when)(copy.start)
        sent.append((copy, when))

    def landed(dst, recv):
        pltpu.make_async_copy(dst, dst, recv_sems.at[recv]).wait()

    barrier = pltpu.get_barrier_semaphore()

    def greet(to_dp, to_node):
        pl.semaphore_signal(barrier, inc=1, device_id={"dp": to_dp, "node": to_node}, device_id_type=MESH)

    for step in range(1, 8):
        greet(dp, lax.rem(node + step, 8))
    greet(at_z(1), node)
    greet(at_z(-1), node)
    greet(pair, node)
    for step in range(1, 4):
        greet(at_side(lax.rem(side + step, 4)), node)
    def last_to(block, cut):
        even = (z + node + 1) % 2
        to_chip = lax.rem(chip + even + 2 * cut, 4)
        return node * 8 + lax.rem(x + block, 4) * 2 + low, to_chip * 2 + par

    def last_from(turn):
        src_chip = z // 2
        even = lax.rem(chip - src_chip + 4, 2)
        src_z = 2 * turn + lax.rem(even + 1 + z, 2)
        src_x = lax.rem(x + 4 - lax.rem(x + core, 2), 4)
        return src_z * 8 + src_x * 2 + low, z

    def is_me(where):
        return jnp.logical_and(where[0] == dp, where[1] == node)

    expected = 13
    for turn in range(4):
        where = last_from(turn)
        pl.when(jnp.logical_not(is_me(where)))(lambda where=where: greet(*where))
    for b in range(2):
        for cut in range(2):
            expected = expected + jnp.where(is_me(last_to(b, cut)), 0, 1)

    for load in loads:
        load.wait()
    eye = lax.broadcasted_iota(jnp.int32, (HID, HID), 0) == lax.broadcasted_iota(jnp.int32, (HID, HID), 1)
    for b in range(WIDE // QB):
        rows = slice(b * QB, (b + 1) * QB)
        line = pl.ds(node * (WIDE // QB) + b, 1)
        w_gu[0, rows, 0:HID] = (gate_codes[rows, :].astype(F32) * gate_scales[line, :]).astype(BF)
        w_gu[0, rows, HID:] = (up_codes[rows, :].astype(F32) * up_scales[line, :]).astype(BF)
        column = jnp.sum(jnp.where(eye, down_scales[line, :], 0.0), axis=1, keepdims=True)
        w_down[0, :, rows] = (down_codes[:, rows].astype(F32) * column).astype(BF)

    pl.semaphore_wait(barrier, expected)

    def quarter_rows(quarter):
        return pl.ds(pl.multiple_of(quarter * CUT, 16), CUT)

    def cols_of(to_node):
        return pl.ds(pl.multiple_of(to_node * WIDE, 128), WIDE)

    is_src = core == par
    fetch_recv = [fresh("recv") for _ in range(3)]
    stage_recv = [fresh("recv") for _ in range(3)]
    own_recv = [fresh("recv") for _ in range(2)]
    own_rows = quarter_rows(z // 2)
    far_steps = (2, 1, 3)
    for a, arr in enumerate((tok, cot)):
        here = jnp.logical_and(is_src, z % 2 == a)
        for step in far_steps:
            push(
                arr.at[own_rows, cols_of(at_chip(step) * 2 + 1 - core)], fetch_buf.at[step - 1],
                stage_recv[step - 1], dp, mate, when=here,
            )
        for step in far_steps:
            to_node = at_chip(step) * 2 + core
            push(
                arr.at[own_rows, cols_of(to_node)], acts_in.at[a, chip, own_rows, :],
                fetch_recv[step - 1], dp, to_node, when=here,
            )

    w_recv = [fresh("recv") for _ in range(2)]
    push(w_gu.at[0], w_gu.at[1], w_recv[0], pair, node)
    push(w_down.at[0], w_down.at[1], w_recv[1], pair, node)

    for a, arr in enumerate((tok, cot)):
        push(arr.at[:, cols_of(mate)], acts_in.at[a, chip], own_recv[a], dp, mate, when=is_src)

        @pl.when(is_src)
        def _(a=a, arr=arr):
            pltpu.make_async_copy(
                arr.at[:, cols_of(node)], acts_in.at[a, chip], recv_sems.at[own_recv[a]]
            ).start()

    not_src = jnp.logical_not(is_src)
    for step in far_steps:
        pl.when(not_src)(lambda step=step: landed(fetch_buf.at[step - 1], stage_recv[step - 1]))
        push(
            fetch_buf.at[step - 1], acts_in.at[z % 2, chip, own_rows, :], fetch_recv[step - 1],
            dp, at_chip(step) * 2 + core, when=not_src,
        )

    up_recv = [[fresh("recv") for _ in range(3)] for _ in range(3)]
    dn_recv = [[fresh("recv") for _ in range(3)] for _ in range(3)]
    far_recv = [fresh("recv") for _ in range(3)]

    def block(turn, step):
        piece = lax.rem(z + turn + 8, 8)
        return acts_in.at[piece % 2, at_chip(-step), quarter_rows(piece // 2), :]

    def relay(turn, step):
        if turn == 0:
            landed(block(0, step), fetch_recv[step - 1])
            push(block(0, step), block(0, step), up_recv[0][step - 1], at_z(1), node)
            push(block(0, step), block(0, step), dn_recv[0][step - 1], at_z(-1), node)
            return
        if turn == 4:
            landed(block(4, step), far_recv[step - 1])
            return
        here = block(-turn, step)
        landed(here, up_recv[turn - 1][step - 1])
        if turn < 3:
            push(here, here, up_recv[turn][step - 1], at_z(1), node)
        elif step != 3:
            push(here, here, far_recv[step - 1], at_z(1), node, when=None if step == 1 else core == 0)
        here = block(turn, step)
        landed(here, dn_recv[turn - 1][step - 1])
        if turn < 3:
            push(here, here, dn_recv[turn][step - 1], at_z(-1), node)
        elif step != 1:
            push(here, here, far_recv[step - 1], at_z(-1), node, when=None if step == 3 else core == 1)

    sign = 1 - 2 * (z % 2)
    quarters = [
        lax.rem(z + first * sign + 8, 8) // 2 for first in (0, -1, 2, -3)
    ]
    mate_recv = [fresh("recv") for _ in range(4)]
    sum_recv = [[fresh("recv") for _ in range(3)] for _ in range(4)]
    hid_recv = [[fresh("recv") for _ in range(3)] for _ in range(4)]
    hid_mate = [[fresh("recv") for _ in range(4)] for _ in range(4)]

    def multiply(s):
        rows = quarter_rows(quarters[s])
        tokens = acts_in[0, :, rows, :].reshape(4 * CUT, WIDE)
        grads = acts_in[1, :, rows, :].reshape(4 * CUT, WIDE)
        for part, store in ((1 - core, other), (core, mine)):
            store[s, :, :, 0 : 2 * HID] = (
                dot_nn(tokens, w_gu[part]).reshape(4, CUT, 2 * HID).astype(store.dtype)
            )
            store[s, :, :, 2 * HID :] = (
                dot_nt(grads, w_down[part]).reshape(4, CUT, HID).astype(store.dtype)
            )
            if store is other:
                push(other.at[s], mate_in.at[s], mate_recv[s], dp, mate)

    def combine(s):
        landed(mate_in.at[s], mate_recv[s])
        for step in far_steps:
            to = at_chip(step)
            sum_out[s, step - 1] = (mine[s, to] + mate_in[s, to].astype(F32)).astype(BF)
            push(
                sum_out.at[s, step - 1], sum_in.at[s, step - 1], sum_recv[s][step - 1],
                dp, to * 2 + core,
            )

    def activate(s):
        full = mine[s, chip] + mate_in[s, chip].astype(F32)
        for i in (0, 2, 1):
            landed(sum_in.at[s, i], sum_recv[s][i])
            full = full + sum_in[s, i].astype(F32)
        rows = quarter_rows(quarters[s])
        gate, upper, d_act = full[:, 0:HID], full[:, HID : 2 * HID], full[:, 2 * HID :]
        sig = jax.nn.sigmoid(gate)
        silu = gate * sig
        hidden[core, chip, rows, 0:HID] = (d_act * upper * sig * (1.0 + gate * (1.0 - sig))).astype(BF)
        hidden[core, chip, rows, HID : 2 * HID] = (d_act * silu).astype(BF)
        hidden[core, chip, rows, 2 * HID :] = (silu * upper).astype(BF)
        own = hidden.at[core, chip, rows]
        for step in far_steps:
            push(own, own, hid_recv[s][step - 1], dp, at_chip(step) * 2 + core)
        push(own, own, hid_mate[s][0], dp, mate)

    def forward_hidden(s):
        rows = quarter_rows(quarters[s])
        for step in (1, 3, 2):
            here = hidden.at[core, at_chip(-step), rows]
            landed(here, hid_recv[s][step - 1])
            push(here, here, hid_mate[s][step], dp, mate)

    def finish_hidden(s):
        rows = quarter_rows(quarters[s])
        for step in range(4):
            landed(hidden.at[1 - core, at_chip(-step), rows], hid_mate[s][step])

    ring_slot = {-3: 0, 3: 1, -2: 2, 2: 3, -1: 4, 1: 5, 0: 6}
    ring_recv = [[fresh("recv") for _ in range(2)] for _ in range(8)]
    buf_slot = {4: 0, 3: 1, -3: 2, 2: 3, -2: 4, 1: 5, -1: 6}
    pairs = ((4, -3), (2, 3), (-2, -1), (0, 1))

    def cut_rows(cut):
        return slice(cut * CUT, (cut + 1) * CUT)

    def token_terms(s, i):
        half = lax.rem(i + z, 2)
        even = lax.rem(half + node + 1, 2)
        rows = quarter_rows(quarters[s])
        total = None
        for part in range(2):
            data = jnp.concatenate(
                [hidden[part, lax.rem(chip + even + 2 * cut, 4), rows, 0 : 2 * HID] for cut in range(2)], axis=0
            )
            term = dot_nt(data, w_gu[part])
            total = term if total is None else total + term
        return total

    def chain(far):
        s, i = [(s, pair.index(far)) for s, pair in enumerate(pairs) if far in pair][0]
        terms = token_terms(s, i)
        if far == 0:
            return terms
        way = 1 if far > 0 else -1
        buf = buf_slot[far]
        for cut in range(2):
            rows = cut_rows(cut)
            value = terms[rows]
            if abs(far) < 3 or far == (-3, 3)[cut]:
                slot = ring_slot[far]
                landed(ring_in.at[slot, rows], ring_recv[slot][cut])
                value = value + ring_in[slot, rows].astype(F32)
            ring_buf[buf, rows] = value.astype(BF)
            if far == 4:
                to, slot = sign * (1 - 2 * cut), (0, 1)[cut]
            else:
                to, slot = sign * way, 7 if far == -1 else ring_slot[-(far - way)]
            push(ring_buf.at[buf, rows], ring_in.at[slot, rows], ring_recv[slot][cut], at_z(to), node)
        return None

    for step in (1, 3, 2):
        relay(0, step)
    relay(1, 1)
    relay(1, 3)
    for a in range(2):
        landed(acts_in.at[a, chip], own_recv[a])
    relay(1, 2)
    landed(w_gu.at[1], w_recv[0])
    landed(w_down.at[1], w_recv[1])
    multiply(0)
    relay(2, 1)
    combine(0)
    relay(2, 3)
    relay(2, 2)
    multiply(1)
    relay(3, 1)
    combine(1)
    relay(3, 3)
    relay(3, 2)
    multiply(2)
    activate(0)
    relay(4, 1)
    combine(2)
    relay(4, 3)
    relay(4, 2)
    multiply(3)
    activate(1)
    combine(3)
    forward_hidden(0)
    activate(2)
    finish_hidden(0)
    chain(4)
    forward_hidden(1)
    activate(3)
    finish_hidden(1)
    chain(-3)
    chain(3)
    chain(2)
    forward_hidden(2)
    finish_hidden(2)
    chain(-2)
    chain(-1)
    forward_hidden(3)
    finish_hidden(3)
    chain(1)

    def weight_grads(part):
        tokens = acts_in[0].reshape(4 * ROWS, WIDE)
        grads = acts_in[1].reshape(4 * ROWS, WIDE)
        back = hidden[part].reshape(4 * ROWS, 3 * HID)
        return dot_tn(tokens, back[:, 0 : 2 * HID]), dot_tn(back[:, 2 * HID :], grads)

    first, second = weight_grads(1)
    grad_out[...] = first.astype(BF)
    down_out[...] = second.astype(BF)
    grad_recv = [fresh("recv") for _ in range(2)]
    push(grad_out, grad_in, grad_recv[0], pair, node)
    push(down_out, down_in, grad_recv[1], pair, node)

    terms = chain(0)

    first, second = weight_grads(0)
    grad_own[...] = first
    down_own[...] = second

    for slot in (7, 6):
        for cut in range(2):
            landed(ring_in.at[slot, cut_rows(cut)], ring_recv[slot][cut])
    terms = terms + ring_in[6].astype(F32) + ring_in[7].astype(F32)
    for i in range(8):
        turn = lax.rem(i // 2 - par + 4, 4)
        member, b = (turn // 2) * 2 + i % 2, lax.rem(turn, 2)
        side_buf[member, b, :, 0:N_COLS] = terms[:, i * N_COLS : (i + 1) * N_COLS].astype(BF)
        side_buf[member, b, :, N_COLS:] = jnp.zeros((96, 128 - N_COLS), BF)

    side_recv = [fresh("recv") for _ in range(3)]
    for step in range(1, 4):
        to = lax.rem(side + step, 4)
        push(side_buf.at[to], side_in.at[step - 1], side_recv[step - 1], at_side(to), node)
    total = side_buf[side].astype(F32)
    for step in range(1, 4):
        landed(side_in.at[step - 1], side_recv[step - 1])
        total = total + side_in[step - 1].astype(F32)
    last_buf[...] = total.astype(BF)

    last_recv = fresh("recv", 4)
    quarter = lax.rem(z // 2 + 2, 4)
    for b in range(2):
        for cut in range(2):
            where = last_to(b, cut)
            src, dst, recv = last_buf.at[b, cut_rows(cut)], last_in.at[quarter], last_recv + quarter
            push(src, dst, recv, *where, when=jnp.logical_not(is_me(where)))

            @pl.when(is_me(where))
            def _(src=src, dst=dst, recv=recv):
                pltpu.make_async_copy(src, dst, recv_sems.at[recv]).start()

    landed(grad_in, grad_recv[0])
    landed(down_in, grad_recv[1])
    gate_grad[...] = (grad_own[:, 0:HID] + grad_in[:, 0:HID].astype(F32)).astype(BF)
    up_grad[...] = (grad_own[:, HID:] + grad_in[:, HID:].astype(F32)).astype(BF)
    down_grad[...] = (down_own[...] + down_in[...].astype(F32)).astype(BF)
    stores = [
        pltpu.make_async_copy(src, dst, store_sems.at[i])
        for i, (src, dst) in enumerate((
            (gate_grad, gate_grad_hbm), (up_grad, up_grad_hbm), (down_grad, down_grad_hbm),
            (token_grad, token_grad_hbm),
        ))
    ]
    for store in stores[:3]:
        store.start()

    for i in range(4):
        landed(last_in.at[i], last_recv + i)
    token_grad[...] = jnp.transpose(last_in[...].reshape(ROWS, 128).astype(F32))[0:N_COLS, :].astype(BF)
    stores[3].start()

    assert max(counts.values()) <= SEMS

    for copy, when in sent:
        if when is None:
            copy.wait_send()
        else:
            pl.when(when)(copy.wait_send)
    for store in stores:
        store.wait()


def write_out(*refs):
    for src, dst in zip(refs[:4], refs[4:]):
        dst[...] = src[...]


def body(tok, cot, gate_codes, up_codes, down_codes, gate_scales, up_scales, down_scales):
    hbm = pl.BlockSpec(memory_space=pltpu.HBM)
    outs = (
        jax.ShapeDtypeStruct((N_COLS, ROWS), BF),
        jax.ShapeDtypeStruct((WIDE, HID), BF),
        jax.ShapeDtypeStruct((WIDE, HID), BF),
        jax.ShapeDtypeStruct((HID, WIDE), BF),
    )
    results = pl.pallas_call(
        kernel,
        out_shape=outs,
        in_specs=[hbm] * 8,
        out_specs=(hbm,) * 4,
        scratch_shapes=[
            pltpu.VMEM((N_COLS, ROWS), BF),
            pltpu.VMEM((WIDE, HID), BF),
            pltpu.VMEM((WIDE, HID), BF),
            pltpu.VMEM((HID, WIDE), BF),
            pltpu.VMEM((WIDE, HID), BF),
            pltpu.VMEM((WIDE, HID), BF),
            pltpu.VMEM((HID, WIDE), BF),
            pltpu.VMEM((40, HID), F32),
            pltpu.VMEM((40, HID), F32),
            pltpu.VMEM((40, HID), F32),
            pltpu.VMEM((2, 4, ROWS, WIDE), BF),
            pltpu.VMEM((3, CUT, WIDE), BF),
            pltpu.VMEM((2, WIDE, 2 * HID), BF),
            pltpu.VMEM((2, HID, WIDE), BF),
            pltpu.VMEM((4, 4, CUT, 3 * HID), F32),
            pltpu.VMEM((4, 4, CUT, 3 * HID), BF),
            pltpu.VMEM((4, 4, CUT, 3 * HID), BF),
            pltpu.VMEM((4, 3, CUT, 3 * HID), BF),
            pltpu.VMEM((4, 3, CUT, 3 * HID), BF),
            pltpu.VMEM((2, 4, ROWS, 3 * HID), BF),
            pltpu.VMEM((WIDE, 2 * HID), BF),
            pltpu.VMEM((HID, WIDE), BF),
            pltpu.VMEM((WIDE, 2 * HID), BF),
            pltpu.VMEM((HID, WIDE), BF),
            pltpu.VMEM((WIDE, 2 * HID), F32),
            pltpu.VMEM((HID, WIDE), F32),
            pltpu.VMEM((7, 96, WIDE), BF),
            pltpu.VMEM((8, 96, WIDE), BF),
            pltpu.VMEM((4, 2, 96, 128), BF),
            pltpu.VMEM((3, 2, 96, 128), BF),
            pltpu.VMEM((2, 96, 128), BF),
            pltpu.VMEM((4, CUT, 128), BF),
            pltpu.SemaphoreType.DMA((6,)),
            pltpu.SemaphoreType.DMA((4,)),
            pltpu.SemaphoreType.DMA((SEMS,)),
            pltpu.SemaphoreType.DMA((SEMS,)),
        ],
        compiler_params=pltpu.CompilerParams(
            collective_id=0, has_side_effects=True, vmem_limit_bytes=VMEM_BYTES
        ),
        cost_estimate=pl.CostEstimate(flops=2_100_000_000, bytes_accessed=5_000_000, transcendentals=25_000),
    )(tok, cot, gate_codes, up_codes, down_codes, gate_scales, up_scales, down_scales.T)
    results = pl.pallas_call(
        write_out,
        out_shape=outs,
        compiler_params=pltpu.CompilerParams(vmem_limit_bytes=VMEM_BYTES),
    )(*results)
    return (results[0].T,) + tuple(results[1:])


def solution(mesh):
    return jax.shard_map(
        body,
        mesh=mesh,
        in_specs=(
            P("node", None),
            P("node", None),
            P("node", "dp"),
            P("node", "dp"),
            P("dp", "node"),
            P(None, "dp"),
            P(None, "dp"),
            P("dp", None),
        ),
        out_specs=(P("node", "dp"), P("node", "dp"), P("node", "dp"), P("dp", "node")),
        check_vma=False,
    )
```

time: 117 us -> 96.1 us (0.82)
  the two profiles are of different devices: /device:TPU:42 before, /device:TPU:58 now
where the time goes in v3:
time: 96.1 us; the launch traced here: 95.9 us
  Pallas kernels  95.3 us (99%)
    pallas_call x1, Pallas kernels, body(): pl.pallas_call(kernel, out_shape=outs, in_specs=[hbm] * 8, out_specs=(hbm...  93.4 us

profile of v3, /device:TPU:58, one launch (start us, length us, event | category | flops | bytes accessed | tf_op | source)
XLA Modules:
  0.0 95.9 jit_solution(8321367704371389413)
XLA Ops:
  0.6 93.4 %shard_map.111 = (bf16[80,192]{1,0:T(8,128)(2,1)}, bf16[640,128]{1,0:T(8,128)(2,1)}, bf16[640,128]{1,0:T(8,128)(2,1)}, bf16[128,640]{1,0:T(8,128)(2,1)}) custom-call(bf16[192,5120]{1,0:T(8,128)(2,1)} %tok.1, bf16[192,5120]{1,0:T(8,128)(2,1)} %cot.1, bf16[640,128]{1,0:T(8,128)(2,1)} %gate_codes_hbm.1, bf16[640,128]{1,0:T(8,128)(2,1)} %up_codes_hbm.1, ...), custom_call_target="tpu_custom_call" | custom-call | flops 2100000000 | bytes 5000000 | tf_op jit(solution)/shard_map/pallas_call | solution.py:465
  94.0 1.9 %shard_map.112 = (bf16[80,192]{1,0:T(8,128)(2,1)}, bf16[640,128]{1,0:T(8,128)(2,1)}, bf16[640,128]{1,0:T(8,128)(2,1)}, bf16[128,640]{1,0:T(8,128)(2,1)}) custom-call(bf16[80,192]{1,0:T(8,128)(2,1)} %get-tuple-element.12.refs_0_, bf16[640,128]{1,0:T(8,128)(2,1)} %get-tuple-element.13.refs_1_, bf16[640,128]{1,0:T(8,128)(2,1)} %get-tuple-element.14.refs_2_, ...), custom_call_target="tpu_custom_call" | custom-call | tf_op jit(solution)/shard_map/pallas_call | solution.py:513

commit v4 on v3

--- a/solution.py
+++ b/solution.py
@@ -100,25 +100,27 @@
         greet(dp, lax.rem(node + step, 8))
     greet(at_z(1), node)
     greet(at_z(-1), node)
+    greet(at_z(4), node)
     greet(pair, node)
     for step in range(1, 4):
         greet(at_side(lax.rem(side + step, 4)), node)
+    def half_at(where, origin):
+        return lax.rem(where - origin + 18, 8) // 4
+
     def last_to(block, cut):
-        even = (z + node + 1) % 2
-        to_chip = lax.rem(chip + even + 2 * cut, 4)
+        to_chip = lax.rem(chip + half_at(z, node) + 2 * cut, 4)
         return node * 8 + lax.rem(x + block, 4) * 2 + low, to_chip * 2 + par
 
-    def last_from(turn):
-        src_chip = z // 2
-        even = lax.rem(chip - src_chip + 4, 2)
-        src_z = 2 * turn + lax.rem(even + 1 + z, 2)
+    def last_from(quarter):
+        half = lax.rem(chip - z // 2 + 4, 2)
+        swap = lax.rem(half_at(quarter + 2, z) + half, 2)
         src_x = lax.rem(x + 4 - lax.rem(x + core, 2), 4)
-        return src_z * 8 + src_x * 2 + low, z
+        return lax.rem(quarter + 2 + 4 * swap, 8) * 8 + src_x * 2 + low, z
 
     def is_me(where):
         return jnp.logical_and(where[0] == dp, where[1] == node)
 
-    expected = 13
+    expected = 14
     for turn in range(4):
         where = last_from(turn)
         pl.when(jnp.logical_not(is_me(where)))(lambda where=where: greet(*where))
@@ -146,24 +148,23 @@
         return pl.ds(pl.multiple_of(to_node * WIDE, 128), WIDE)
 
     is_src = core == par
-    fetch_recv = [fresh("recv") for _ in range(3)]
-    stage_recv = [fresh("recv") for _ in range(3)]
+    fetch_recv = [[fresh("recv") for _ in range(3)] for _ in range(2)]
+    stage_recv = [[fresh("recv") for _ in range(3)] for _ in range(2)]
     own_recv = [fresh("recv") for _ in range(2)]
-    own_rows = quarter_rows(z // 2)
+    own_rows = quarter_rows(z % 4)
     far_steps = (2, 1, 3)
-    for a, arr in enumerate((tok, cot)):
-        here = jnp.logical_and(is_src, z % 2 == a)
-        for step in far_steps:
-            push(
-                arr.at[own_rows, cols_of(at_chip(step) * 2 + 1 - core)], fetch_buf.at[step - 1],
-                stage_recv[step - 1], dp, mate, when=here,
-            )
-        for step in far_steps:
-            to_node = at_chip(step) * 2 + core
-            push(
-                arr.at[own_rows, cols_of(to_node)], acts_in.at[a, chip, own_rows, :],
-                fetch_recv[step - 1], dp, to_node, when=here,
-            )
+    items = ((0, 1), (1, 3), (1, 1), (0, 3), (0, 2), (1, 2))
+    for a, step in items:
+        push(
+            (tok, cot)[a].at[own_rows, cols_of(at_chip(step) * 2 + 1 - core)], fetch_buf.at[a, step - 1],
+            stage_recv[a][step - 1], dp, mate, when=is_src,
+        )
+    for a, step in items:
+        to_node = at_chip(step) * 2 + core
+        push(
+            (tok, cot)[a].at[own_rows, cols_of(to_node)], acts_in.at[a, chip, own_rows, :],
+            fetch_recv[a][step - 1], dp, to_node, when=is_src,
+        )
 
     w_recv = [fresh("recv") for _ in range(2)]
     push(w_gu.at[0], w_gu.at[1], w_recv[0], pair, node)
@@ -179,47 +180,41 @@
             ).start()
 
     not_src = jnp.logical_not(is_src)
-    for step in far_steps:
-        pl.when(not_src)(lambda step=step: landed(fetch_buf.at[step - 1], stage_recv[step - 1]))
+    for a, step in items:
+        pl.when(not_src)(lambda a=a, step=step: landed(fetch_buf.at[a, step - 1], stage_recv[a][step - 1]))
         push(
-            fetch_buf.at[step - 1], acts_in.at[z % 2, chip, own_rows, :], fetch_recv[step - 1],
+            fetch_buf.at[a, step - 1], acts_in.at[a, chip, own_rows, :], fetch_recv[a][step - 1],
             dp, at_chip(step) * 2 + core, when=not_src,
         )
 
-    up_recv = [[fresh("recv") for _ in range(3)] for _ in range(3)]
-    dn_recv = [[fresh("recv") for _ in range(3)] for _ in range(3)]
-    far_recv = [fresh("recv") for _ in range(3)]
-
-    def block(turn, step):
-        piece = lax.rem(z + turn + 8, 8)
-        return acts_in.at[piece % 2, at_chip(-step), quarter_rows(piece // 2), :]
-
-    def relay(turn, step):
+    up_recv = [[fresh("recv") for _ in range(3)] for _ in range(2)]
+    dn_recv = [[fresh("recv") for _ in range(3)] for _ in range(2)]
+    far_recv = [[fresh("recv") for _ in range(3)] for _ in range(2)]
+
+    def block(turn, item):
+        a, step = items[item]
+        return acts_in.at[a, at_chip(-step), quarter_rows(lax.rem(z + turn + 4, 4)), :]
+
+    def relay(turn, item):
+        a, step = items[item]
         if turn == 0:
-            landed(block(0, step), fetch_recv[step - 1])
-            push(block(0, step), block(0, step), up_recv[0][step - 1], at_z(1), node)
-            push(block(0, step), block(0, step), dn_recv[0][step - 1], at_z(-1), node)
-            return
-        if turn == 4:
-            landed(block(4, step), far_recv[step - 1])
-            return
-        here = block(-turn, step)
-        landed(here, up_recv[turn - 1][step - 1])
-        if turn < 3:
-            push(here, here, up_recv[turn][step - 1], at_z(1), node)
-        elif step != 3:
-            push(here, here, far_recv[step - 1], at_z(1), node, when=None if step == 1 else core == 0)
-        here = block(turn, step)
-        landed(here, dn_recv[turn - 1][step - 1])
-        if turn < 3:
-            push(here, here, dn_recv[turn][step - 1], at_z(-1), node)
-        elif step != 1:
-            push(here, here, far_recv[step - 1], at_z(-1), node, when=None if step == 3 else core == 1)
-
-    sign = 1 - 2 * (z % 2)
-    quarters = [
-        lax.rem(z + first * sign + 8, 8) // 2 for first in (0, -1, 2, -3)
-    ]
+            here = block(0, item)
+            landed(here, fetch_recv[a][step - 1])
+            push(here, here, up_recv[a][step - 1], at_z(1), node)
+            push(here, here, dn_recv[a][step - 1], at_z(-1), node)
+        elif turn == 1:
+            here = block(-1, item)
+            landed(here, up_recv[a][step - 1])
+            if a == 0:
+                push(here, here, far_recv[a][step - 1], at_z(1), node)
+            here = block(1, item)
+            landed(here, dn_recv[a][step - 1])
+            if a == 1:
+                push(here, here, far_recv[a][step - 1], at_z(-1), node)
+        else:
+            landed(block(2, item), far_recv[a][step - 1])
+
+    quarters = [lax.rem(z + turn, 4) for turn in (0, 1, 3, 2)]
     mate_recv = [fresh("recv") for _ in range(4)]
     sum_recv = [[fresh("recv") for _ in range(3)] for _ in range(4)]
     hid_recv = [[fresh("recv") for _ in range(3)] for _ in range(4)]
@@ -278,94 +273,90 @@
         for step in range(4):
             landed(hidden.at[1 - core, at_chip(-step), rows], hid_mate[s][step])
 
-    ring_slot = {-3: 0, 3: 1, -2: 2, 2: 3, -1: 4, 1: 5, 0: 6}
-    ring_recv = [[fresh("recv") for _ in range(2)] for _ in range(8)]
+    ring_slot = {2: 0, 1: 1, -2: 2, -1: 3, (0, 1): 4, (0, -1): 5, (0, 4): 6}
+    ring_recv = [[fresh("recv") for _ in range(2)] for _ in range(7)]
     buf_slot = {4: 0, 3: 1, -3: 2, 2: 3, -2: 4, 1: 5, -1: 6}
-    pairs = ((4, -3), (2, 3), (-2, -1), (0, 1))
+    pairs = ((2, -2), (3, -1), (1, -3), (4, 0))
 
     def cut_rows(cut):
         return slice(cut * CUT, (cut + 1) * CUT)
 
-    def token_terms(s, i):
-        half = lax.rem(i + z, 2)
-        even = lax.rem(half + node + 1, 2)
+    def token_terms(s, far):
+        half = half_at(z + far, node)
         rows = quarter_rows(quarters[s])
         total = None
         for part in range(2):
             data = jnp.concatenate(
-                [hidden[part, lax.rem(chip + even + 2 * cut, 4), rows, 0 : 2 * HID] for cut in range(2)], axis=0
+                [hidden[part, lax.rem(chip + half + 2 * cut, 4), rows, 0 : 2 * HID] for cut in range(2)], axis=0
             )
             term = dot_nt(data, w_gu[part])
             total = term if total is None else total + term
         return total
 
     def chain(far):
-        s, i = [(s, pair.index(far)) for s, pair in enumerate(pairs) if far in pair][0]
-        terms = token_terms(s, i)
+        s = [s for s, pair in enumerate(pairs) if far in pair][0]
+        terms = token_terms(s, far)
         if far == 0:
             return terms
         way = 1 if far > 0 else -1
-        buf = buf_slot[far]
+        to, buf = (4 if far == 4 else way), buf_slot[far]
+        into = ring_slot[far - way] if 1 < abs(far) < 4 else ring_slot[0, far]
         for cut in range(2):
             rows = cut_rows(cut)
             value = terms[rows]
-            if abs(far) < 3 or far == (-3, 3)[cut]:
+            if abs(far) < 3:
                 slot = ring_slot[far]
                 landed(ring_in.at[slot, rows], ring_recv[slot][cut])
                 value = value + ring_in[slot, rows].astype(F32)
             ring_buf[buf, rows] = value.astype(BF)
-            if far == 4:
-                to, slot = sign * (1 - 2 * cut), (0, 1)[cut]
-            else:
-                to, slot = sign * way, 7 if far == -1 else ring_slot[-(far - way)]
-            push(ring_buf.at[buf, rows], ring_in.at[slot, rows], ring_recv[slot][cut], at_z(to), node)
+            push(ring_buf.at[buf, rows], ring_in.at[into, rows], ring_recv[into][cut], at_z(to), node)
         return None
 
-    for step in (1, 3, 2):
-        relay(0, step)
+    relay(0, 0)
+    relay(0, 1)
+    relay(0, 2)
+    relay(1, 0)
+    relay(0, 3)
     relay(1, 1)
-    relay(1, 3)
+    relay(0, 4)
+    relay(1, 2)
+    relay(0, 5)
     for a in range(2):
         landed(acts_in.at[a, chip], own_recv[a])
-    relay(1, 2)
     landed(w_gu.at[1], w_recv[0])
     landed(w_down.at[1], w_recv[1])
     multiply(0)
-    relay(2, 1)
+    relay(1, 3)
+    relay(1, 4)
     combine(0)
-    relay(2, 3)
-    relay(2, 2)
+    relay(1, 5)
     multiply(1)
-    relay(3, 1)
+    multiply(2)
     combine(1)
-    relay(3, 3)
-    relay(3, 2)
-    multiply(2)
+    combine(2)
+    for item in range(6):
+        relay(2, item)
+    multiply(3)
     activate(0)
-    relay(4, 1)
-    combine(2)
-    relay(4, 3)
-    relay(4, 2)
-    multiply(3)
-    activate(1)
     combine(3)
     forward_hidden(0)
+    activate(1)
     activate(2)
     finish_hidden(0)
-    chain(4)
     forward_hidden(1)
     activate(3)
+    forward_hidden(2)
     finish_hidden(1)
+    chain(3)
+    finish_hidden(2)
     chain(-3)
-    chain(3)
     chain(2)
-    forward_hidden(2)
-    finish_hidden(2)
+    forward_hidden(3)
+    chain(1)
     chain(-2)
+    finish_hidden(3)
+    chain(4)
     chain(-1)
-    forward_hidden(3)
-    finish_hidden(3)
-    chain(1)
 
     def weight_grads(part):
         tokens = acts_in[0].reshape(4 * ROWS, WIDE)
@@ -386,10 +377,10 @@
     grad_own[...] = first
     down_own[...] = second
 
-    for slot in (7, 6):
+    for slot in (4, 5, 6):
         for cut in range(2):
             landed(ring_in.at[slot, cut_rows(cut)], ring_recv[slot][cut])
-    terms = terms + ring_in[6].astype(F32) + ring_in[7].astype(F32)
+        terms = terms + ring_in[slot].astype(F32)
     for i in range(8):
         turn = lax.rem(i // 2 - par + 4, 4)
         member, b = (turn // 2) * 2 + i % 2, lax.rem(turn, 2)
@@ -407,7 +398,7 @@
     last_buf[...] = total.astype(BF)
 
     last_recv = fresh("recv", 4)
-    quarter = lax.rem(z // 2 + 2, 4)
+    quarter = lax.rem(z + 2, 4)
     for b in range(2):
         for cut in range(2):
             where = last_to(b, cut)
@@ -479,7 +470,7 @@
             pltpu.VMEM((40, HID), F32),
             pltpu.VMEM((40, HID), F32),
             pltpu.VMEM((2, 4, ROWS, WIDE), BF),
-            pltpu.VMEM((3, CUT, WIDE), BF),
+            pltpu.VMEM((2, 3, CUT, WIDE), BF),
             pltpu.VMEM((2, WIDE, 2 * HID), BF),
             pltpu.VMEM((2, HID, WIDE), BF),
             pltpu.VMEM((4, 4, CUT, 3 * HID), F32),
@@ -495,7 +486,7 @@
             pltpu.VMEM((WIDE, 2 * HID), F32),
             pltpu.VMEM((HID, WIDE), F32),
             pltpu.VMEM((7, 96, WIDE), BF),
-            pltpu.VMEM((8, 96, WIDE), BF),
+            pltpu.VMEM((7, 96, WIDE), BF),
             pltpu.VMEM((4, 2, 96, 128), BF),
             pltpu.VMEM((3, 2, 96, 128), BF),
             pltpu.VMEM((2, 96, 128), BF),

time: 96.1 us -> 108 us (1.12)
  the two profiles are of different devices: /device:TPU:58 before, /device:TPU:18 now
where the time goes in v4:
time: 108 us
  Pallas kernels  108 us (100%)
    pallas_call x1, Pallas kernels, body(): pl.pallas_call(kernel, out_shape=outs, in_specs=[hbm] * 8, out_specs=(hbm...  106 us

profile of v4, /device:TPU:18, one launch (start us, length us, event | category | flops | bytes accessed | tf_op | source)
XLA Modules:
  0.0 108.3 jit_solution(4763306795846466492)
XLA Ops:
  0.6 105.8 %shard_map.111 = (bf16[80,192]{1,0:T(8,128)(2,1)}, bf16[640,128]{1,0:T(8,128)(2,1)}, bf16[640,128]{1,0:T(8,128)(2,1)}, bf16[128,640]{1,0:T(8,128)(2,1)}) custom-call(bf16[192,5120]{1,0:T(8,128)(2,1)} %tok.1, bf16[192,5120]{1,0:T(8,128)(2,1)} %cot.1, bf16[640,128]{1,0:T(8,128)(2,1)} %gate_codes_hbm.1, bf16[640,128]{1,0:T(8,128)(2,1)} %up_codes_hbm.1, ...), custom_call_target="tpu_custom_call" | custom-call | flops 2100000000 | bytes 5000000 | tf_op jit(solution)/shard_map/pallas_call | solution.py:456
  106.4 1.9 %shard_map.112 = (bf16[80,192]{1,0:T(8,128)(2,1)}, bf16[640,128]{1,0:T(8,128)(2,1)}, bf16[640,128]{1,0:T(8,128)(2,1)}, bf16[128,640]{1,0:T(8,128)(2,1)}) custom-call(bf16[80,192]{1,0:T(8,128)(2,1)} %get-tuple-element.12.refs_0_, bf16[640,128]{1,0:T(8,128)(2,1)} %get-tuple-element.13.refs_1_, bf16[640,128]{1,0:T(8,128)(2,1)} %get-tuple-element.14.refs_2_, ...), custom_call_target="tpu_custom_call" | custom-call | tf_op jit(solution)/shard_map/pallas_call | solution.py:504

commit v5 on v3

--- a/solution.py
+++ b/solution.py
@@ -103,39 +103,17 @@
     greet(pair, node)
     for step in range(1, 4):
         greet(at_side(lax.rem(side + step, 4)), node)
+    def odd_half(where, origin):
+        return lax.rem(lax.rem(where - where % 2 - origin + 16, 8) // 4 + where, 2)
+
     def last_to(block, cut):
-        even = (z + node + 1) % 2
-        to_chip = lax.rem(chip + even + 2 * cut, 4)
+        to_chip = lax.rem(chip + odd_half(z, node) + 2 * cut, 4)
         return node * 8 + lax.rem(x + block, 4) * 2 + low, to_chip * 2 + par
-
-    def last_from(turn):
-        src_chip = z // 2
-        even = lax.rem(chip - src_chip + 4, 2)
-        src_z = 2 * turn + lax.rem(even + 1 + z, 2)
-        src_x = lax.rem(x + 4 - lax.rem(x + core, 2), 4)
-        return src_z * 8 + src_x * 2 + low, z
 
     def is_me(where):
         return jnp.logical_and(where[0] == dp, where[1] == node)
 
     expected = 13
-    for turn in range(4):
-        where = last_from(turn)
-        pl.when(jnp.logical_not(is_me(where)))(lambda where=where: greet(*where))
-    for b in range(2):
-        for cut in range(2):
-            expected = expected + jnp.where(is_me(last_to(b, cut)), 0, 1)
-
-    for load in loads:
-        load.wait()
-    eye = lax.broadcasted_iota(jnp.int32, (HID, HID), 0) == lax.broadcasted_iota(jnp.int32, (HID, HID), 1)
-    for b in range(WIDE // QB):
-        rows = slice(b * QB, (b + 1) * QB)
-        line = pl.ds(node * (WIDE // QB) + b, 1)
-        w_gu[0, rows, 0:HID] = (gate_codes[rows, :].astype(F32) * gate_scales[line, :]).astype(BF)
-        w_gu[0, rows, HID:] = (up_codes[rows, :].astype(F32) * up_scales[line, :]).astype(BF)
-        column = jnp.sum(jnp.where(eye, down_scales[line, :], 0.0), axis=1, keepdims=True)
-        w_down[0, :, rows] = (down_codes[:, rows].astype(F32) * column).astype(BF)
 
     pl.semaphore_wait(barrier, expected)
 
@@ -165,10 +143,6 @@
                 fetch_recv[step - 1], dp, to_node, when=here,
             )
 
-    w_recv = [fresh("recv") for _ in range(2)]
-    push(w_gu.at[0], w_gu.at[1], w_recv[0], pair, node)
-    push(w_down.at[0], w_down.at[1], w_recv[1], pair, node)
-
     for a, arr in enumerate((tok, cot)):
         push(arr.at[:, cols_of(mate)], acts_in.at[a, chip], own_recv[a], dp, mate, when=is_src)
 
@@ -185,6 +159,21 @@
             fetch_buf.at[step - 1], acts_in.at[z % 2, chip, own_rows, :], fetch_recv[step - 1],
             dp, at_chip(step) * 2 + core, when=not_src,
         )
+
+    for load in loads:
+        load.wait()
+    eye = lax.broadcasted_iota(jnp.int32, (HID, HID), 0) == lax.broadcasted_iota(jnp.int32, (HID, HID), 1)
+    for b in range(WIDE // QB):
+        rows = slice(b * QB, (b + 1) * QB)
+        line = pl.ds(node * (WIDE // QB) + b, 1)
+        w_gu[0, rows, 0:HID] = (gate_codes[rows, :].astype(F32) * gate_scales[line, :]).astype(BF)
+        w_gu[0, rows, HID:] = (up_codes[rows, :].astype(F32) * up_scales[line, :]).astype(BF)
+        column = jnp.sum(jnp.where(eye, down_scales[line, :], 0.0), axis=1, keepdims=True)
+        w_down[0, :, rows] = (down_codes[:, rows].astype(F32) * column).astype(BF)
+
+    w_recv = [fresh("recv") for _ in range(2)]
+    push(w_gu.at[0], w_gu.at[1], w_recv[0], pair, node)
+    push(w_down.at[0], w_down.at[1], w_recv[1], pair, node)
 
     up_recv = [[fresh("recv") for _ in range(3)] for _ in range(3)]
     dn_recv = [[fresh("recv") for _ in range(3)] for _ in range(3)]
@@ -287,13 +276,12 @@
         return slice(cut * CUT, (cut + 1) * CUT)
 
     def token_terms(s, i):
-        half = lax.rem(i + z, 2)
-        even = lax.rem(half + node + 1, 2)
         rows = quarter_rows(quarters[s])
+        half = odd_half(lax.rem(2 * quarters[s] + 4, 8) + lax.rem(i + z, 2), node)
         total = None
         for part in range(2):
             data = jnp.concatenate(
-                [hidden[part, lax.rem(chip + even + 2 * cut, 4), rows, 0 : 2 * HID] for cut in range(2)], axis=0
+                [hidden[part, lax.rem(chip + half + 2 * cut, 4), rows, 0 : 2 * HID] for cut in range(2)], axis=0
             )
             term = dot_nt(data, w_gu[part])
             total = term if total is None else total + term
@@ -352,20 +340,23 @@
     forward_hidden(0)
     activate(2)
     finish_hidden(0)
+    forward_hidden(1)
     chain(4)
-    forward_hidden(1)
     activate(3)
     finish_hidden(1)
+    forward_hidden(2)
     chain(-3)
     chain(3)
+    finish_hidden(2)
+    forward_hidden(3)
     chain(2)
-    forward_hidden(2)
-    finish_hidden(2)
     chain(-2)
+    finish_hidden(3)
     chain(-1)
-    forward_hidden(3)
-    finish_hidden(3)
     chain(1)
+
+    def cols(b):
+        return slice(b * HID, (b + 1) * HID)
 
     def weight_grads(part):
         tokens = acts_in[0].reshape(4 * ROWS, WIDE)
@@ -376,9 +367,8 @@
     first, second = weight_grads(1)
     grad_out[...] = first.astype(BF)
     down_out[...] = second.astype(BF)
-    grad_recv = [fresh("recv") for _ in range(2)]
-    push(grad_out, grad_in, grad_recv[0], pair, node)
-    push(down_out, down_in, grad_recv[1], pair, node)
+    grad_recv = [fresh("recv") for _ in range(3)]
+    push(down_out, down_in, grad_recv[0], pair, node)
 
     terms = chain(0)
 
@@ -400,6 +390,8 @@
     for step in range(1, 4):
         to = lax.rem(side + step, 4)
         push(side_buf.at[to], side_in.at[step - 1], side_recv[step - 1], at_side(to), node)
+    for b in range(2):
+        push(grad_out.at[:, cols(b)], grad_in.at[:, cols(b)], grad_recv[1 + b], pair, node)
     total = side_buf[side].astype(F32)
     for step in range(1, 4):
         landed(side_in.at[step - 1], side_recv[step - 1])
@@ -418,8 +410,9 @@
             def _(src=src, dst=dst, recv=recv):
                 pltpu.make_async_copy(src, dst, recv_sems.at[recv]).start()
 
-    landed(grad_in, grad_recv[0])
-    landed(down_in, grad_recv[1])
+    landed(down_in, grad_recv[0])
+    for b in range(2):
+        landed(grad_in.at[:, cols(b)], grad_recv[1 + b])
     gate_grad[...] = (grad_own[:, 0:HID] + grad_in[:, 0:HID].astype(F32)).astype(BF)
     up_grad[...] = (grad_own[:, HID:] + grad_in[:, HID:].astype(F32)).astype(BF)
     down_grad[...] = (down_own[...] + down_in[...].astype(F32)).astype(BF)

time: 96.1 us -> 90.6 us (0.943)
  the two profiles are of different devices: /device:TPU:58 before, /device:TPU:2 now
where the time goes in v5:
time: 90.6 us; the launch traced here: 90.5 us
  Pallas kernels  89.8 us (99%)
    pallas_call x1, Pallas kernels, body(): pl.pallas_call(kernel, out_shape=outs, in_specs=[hbm] * 8, out_specs=(hbm...  87.9 us
    pallas_call x1, Pallas kernels, body(): pl.pallas_call(write_out, out_shape=outs, compiler_params=pltpu.CompilerP...  1.9 us

profile of v5, /device:TPU:2, one launch (start us, length us, event | category | flops | bytes accessed | tf_op | source)
XLA Modules:
  0.0 90.5 jit_solution(11205882058501067734)
XLA Ops:
  0.6 87.9 %shard_map.111 = (bf16[80,192]{1,0:T(8,128)(2,1)}, bf16[640,128]{1,0:T(8,128)(2,1)}, bf16[640,128]{1,0:T(8,128)(2,1)}, bf16[128,640]{1,0:T(8,128)(2,1)}) custom-call(bf16[192,5120]{1,0:T(8,128)(2,1)} %tok.1, bf16[192,5120]{1,0:T(8,128)(2,1)} %cot.1, bf16[640,128]{1,0:T(8,128)(2,1)} %gate_codes_hbm.1, bf16[640,128]{1,0:T(8,128)(2,1)} %up_codes_hbm.1, ...), custom_call_target="tpu_custom_call" | custom-call | flops 2100000000 | bytes 5000000 | tf_op jit(solution)/shard_map/pallas_call | solution.py:458
  88.6 1.9 %shard_map.112 = (bf16[80,192]{1,0:T(8,128)(2,1)}, bf16[640,128]{1,0:T(8,128)(2,1)}, bf16[640,128]{1,0:T(8,128)(2,1)}, bf16[128,640]{1,0:T(8,128)(2,1)}) custom-call(bf16[80,192]{1,0:T(8,128)(2,1)} %get-tuple-element.12.refs_0_, bf16[640,128]{1,0:T(8,128)(2,1)} %get-tuple-element.13.refs_1_, bf16[640,128]{1,0:T(8,128)(2,1)} %get-tuple-element.14.refs_2_, ...), custom_call_target="tpu_custom_call" | custom-call | tf_op jit(solution)/shard_map/pallas_call | solution.py:506

commit v6 on v5

--- a/solution.py
+++ b/solution.py
@@ -15,7 +15,8 @@
 QB = 128
 CUT = 48
 VMEM_BYTES = 60 * 1024 * 1024
-SEMS = 144
+SEMS = 160
+RELAYED = (0, 1, 2, 3)
 N_COLS = 80
 
 
@@ -212,6 +213,12 @@
     mate_recv = [fresh("recv") for _ in range(4)]
     sum_recv = [[fresh("recv") for _ in range(3)] for _ in range(4)]
     hid_recv = [[fresh("recv") for _ in range(3)] for _ in range(4)]
+    hid_far = [[fresh("recv") for _ in range(3)] for _ in range(4)]
+    ways = (1, 1 - 2 * core, -1)
+
+    def cols(b):
+        return slice(b * HID, (b + 1) * HID)
+
     hid_mate = [[fresh("recv") for _ in range(4)] for _ in range(4)]
 
     def multiply(s):
@@ -251,16 +258,27 @@
         hidden[core, chip, rows, HID : 2 * HID] = (d_act * silu).astype(BF)
         hidden[core, chip, rows, 2 * HID :] = (silu * upper).astype(BF)
         own = hidden.at[core, chip, rows]
-        for step in far_steps:
+        for step in (1, 3) if s in RELAYED else far_steps:
             push(own, own, hid_recv[s][step - 1], dp, at_chip(step) * 2 + core)
         push(own, own, hid_mate[s][0], dp, mate)
 
     def forward_hidden(s):
         rows = quarter_rows(quarters[s])
-        for step in (1, 3, 2):
+        for step in (1, 3) if s in RELAYED else (1, 3, 2):
             here = hidden.at[core, at_chip(-step), rows]
             landed(here, hid_recv[s][step - 1])
             push(here, here, hid_mate[s][step], dp, mate)
+        if s in RELAYED:
+            for b in range(3):
+                here = hidden.at[core, at_chip(-ways[b]), rows, cols(b)]
+                push(here, here, hid_far[s][b], dp, at_chip(ways[b]) * 2 + core)
+
+    def last_hidden(s):
+        rows = quarter_rows(quarters[s])
+        for b in range(3):
+            landed(hidden.at[core, at_chip(2), rows, cols(b)], hid_far[s][b])
+        here = hidden.at[core, at_chip(2), rows]
+        push(here, here, hid_mate[s][2], dp, mate)
 
     def finish_hidden(s):
         rows = quarter_rows(quarters[s])
@@ -339,24 +357,25 @@
     combine(3)
     forward_hidden(0)
     activate(2)
+    forward_hidden(1)
+    last_hidden(0)
+    activate(3)
     finish_hidden(0)
-    forward_hidden(1)
     chain(4)
-    activate(3)
+    forward_hidden(2)
+    last_hidden(1)
     finish_hidden(1)
-    forward_hidden(2)
     chain(-3)
     chain(3)
+    last_hidden(2)
+    forward_hidden(3)
     finish_hidden(2)
-    forward_hidden(3)
+    last_hidden(3)
     chain(2)
     chain(-2)
     finish_hidden(3)
     chain(-1)
     chain(1)
-
-    def cols(b):
-        return slice(b * HID, (b + 1) * HID)
 
     def weight_grads(part):
         tokens = acts_in[0].reshape(4 * ROWS, WIDE)

time: 90.6 us -> 88.2 us (0.974)
  the two profiles are of different devices: /device:TPU:2 before, /device:TPU:1 now
where the time goes in v6:
time: 88.2 us; the launch traced here: 88.1 us
  Pallas kernels  87.4 us (99%)
    pallas_call x1, Pallas kernels, body(): pl.pallas_call(kernel, out_shape=outs, in_specs=[hbm] * 8, out_specs=(hbm...  85.5 us
    pallas_call x1, Pallas kernels, body(): pl.pallas_call(write_out, out_shape=outs, compiler_params=pltpu.CompilerP...  1.9 us

profile of v6, /device:TPU:1, one launch (start us, length us, event | category | flops | bytes accessed | tf_op | source)
XLA Modules:
  0.0 88.1 jit_solution(5469220237693413677)
XLA Ops:
  0.6 85.5 %shard_map.111 = (bf16[80,192]{1,0:T(8,128)(2,1)}, bf16[640,128]{1,0:T(8,128)(2,1)}, bf16[640,128]{1,0:T(8,128)(2,1)}, bf16[128,640]{1,0:T(8,128)(2,1)}) custom-call(bf16[192,5120]{1,0:T(8,128)(2,1)} %tok.1, bf16[192,5120]{1,0:T(8,128)(2,1)} %cot.1, bf16[640,128]{1,0:T(8,128)(2,1)} %gate_codes_hbm.1, bf16[640,128]{1,0:T(8,128)(2,1)} %up_codes_hbm.1, ...), custom_call_target="tpu_custom_call" | custom-call | flops 2100000000 | bytes 5000000 | tf_op jit(solution)/shard_map/pallas_call | solution.py:477
  86.2 1.9 %shard_map.112 = (bf16[80,192]{1,0:T(8,128)(2,1)}, bf16[640,128]{1,0:T(8,128)(2,1)}, bf16[640,128]{1,0:T(8,128)(2,1)}, bf16[128,640]{1,0:T(8,128)(2,1)}) custom-call(bf16[80,192]{1,0:T(8,128)(2,1)} %get-tuple-element.12.refs_0_, bf16[640,128]{1,0:T(8,128)(2,1)} %get-tuple-element.13.refs_1_, bf16[640,128]{1,0:T(8,128)(2,1)} %get-tuple-element.14.refs_2_, ...), custom_call_target="tpu_custom_call" | custom-call | tf_op jit(solution)/shard_map/pallas_call | solution.py:525

commit v7 on v6

--- a/solution.py
+++ b/solution.py
@@ -239,19 +239,24 @@
         landed(mate_in.at[s], mate_recv[s])
         for step in far_steps:
             to = at_chip(step)
-            sum_out[s, step - 1] = (mine[s, to] + mate_in[s, to].astype(F32)).astype(BF)
+            total = mine[s, to] + mate_in[s, to]
+            high = total.astype(BF)
+            sum_out[s, step - 1, :, 0 : 3 * HID] = high
+            sum_out[s, step - 1, :, 3 * HID :] = (total[:, 0:HID] - high[:, 0:HID].astype(F32)).astype(BF)
             push(
                 sum_out.at[s, step - 1], sum_in.at[s, step - 1], sum_recv[s][step - 1],
                 dp, to * 2 + core,
             )
 
     def activate(s):
-        full = mine[s, chip] + mate_in[s, chip].astype(F32)
+        full = mine[s, chip] + mate_in[s, chip]
+        rest = jnp.zeros((CUT, HID), F32)
         for i in (0, 2, 1):
             landed(sum_in.at[s, i], sum_recv[s][i])
-            full = full + sum_in[s, i].astype(F32)
+            full = full + sum_in[s, i, :, 0 : 3 * HID].astype(F32)
+            rest = rest + sum_in[s, i, :, 3 * HID :].astype(F32)
         rows = quarter_rows(quarters[s])
-        gate, upper, d_act = full[:, 0:HID], full[:, HID : 2 * HID], full[:, 2 * HID :]
+        gate, upper, d_act = full[:, 0:HID] + rest, full[:, HID : 2 * HID], full[:, 2 * HID :]
         sig = jax.nn.sigmoid(gate)
         silu = gate * sig
         hidden[core, chip, rows, 0:HID] = (d_act * upper * sig * (1.0 + gate * (1.0 - sig))).astype(BF)
@@ -267,11 +272,15 @@
         for step in (1, 3) if s in RELAYED else (1, 3, 2):
             here = hidden.at[core, at_chip(-step), rows]
             landed(here, hid_recv[s][step - 1])
-            push(here, here, hid_mate[s][step], dp, mate)
+            if s not in RELAYED:
+                push(here, here, hid_mate[s][step], dp, mate)
         if s in RELAYED:
             for b in range(3):
                 here = hidden.at[core, at_chip(-ways[b]), rows, cols(b)]
                 push(here, here, hid_far[s][b], dp, at_chip(ways[b]) * 2 + core)
+            for step in (1, 3):
+                here = hidden.at[core, at_chip(-step), rows]
+                push(here, here, hid_mate[s][step], dp, mate)
 
     def last_hidden(s):
         rows = quarter_rows(quarters[s])
@@ -495,10 +504,10 @@
             pltpu.VMEM((2, WIDE, 2 * HID), BF),
             pltpu.VMEM((2, HID, WIDE), BF),
             pltpu.VMEM((4, 4, CUT, 3 * HID), F32),
-            pltpu.VMEM((4, 4, CUT, 3 * HID), BF),
-            pltpu.VMEM((4, 4, CUT, 3 * HID), BF),
-            pltpu.VMEM((4, 3, CUT, 3 * HID), BF),
-            pltpu.VMEM((4, 3, CUT, 3 * HID), BF),
+            pltpu.VMEM((4, 4, CUT, 3 * HID), F32),
+            pltpu.VMEM((4, 4, CUT, 3 * HID), F32),
+            pltpu.VMEM((4, 3, CUT, 4 * HID), BF),
+            pltpu.VMEM((4, 3, CUT, 4 * HID), BF),
             pltpu.VMEM((2, 4, ROWS, 3 * HID), BF),
             pltpu.VMEM((WIDE, 2 * HID), BF),
             pltpu.VMEM((HID, WIDE), BF),

time: 88.2 us -> 93.3 us (1.058)
  Pallas kernels: 87.4 us -> 92.1 us
    pallas_call x1, Pallas kernels: 85.5 us -> 90.2 us  [body(): pl.pallas_call(kernel, out_shape=outs, in_specs=[hbm] * 8, out_specs=(hbm...]
where the time goes in v7:
time: 93.3 us; the launch traced here: 92.7 us
  Pallas kernels  92.1 us (99%)
    pallas_call x1, Pallas kernels, body(): pl.pallas_call(kernel, out_shape=outs, in_specs=[hbm] * 8, out_specs=(hbm...  90.2 us
    pallas_call x1, Pallas kernels, body(): pl.pallas_call(write_out, out_shape=outs, compiler_params=pltpu.CompilerP...  1.9 us

profile of v7, /device:TPU:1, one launch (start us, length us, event | category | flops | bytes accessed | tf_op | source)
XLA Modules:
  0.0 92.7 jit_solution(114119678705865853)
XLA Ops:
  0.6 90.2 %shard_map.111 = (bf16[80,192]{1,0:T(8,128)(2,1)}, bf16[640,128]{1,0:T(8,128)(2,1)}, bf16[640,128]{1,0:T(8,128)(2,1)}, bf16[128,640]{1,0:T(8,128)(2,1)}) custom-call(bf16[192,5120]{1,0:T(8,128)(2,1)} %tok.1, bf16[192,5120]{1,0:T(8,128)(2,1)} %cot.1, bf16[640,128]{1,0:T(8,128)(2,1)} %gate_codes_hbm.1, bf16[640,128]{1,0:T(8,128)(2,1)} %up_codes_hbm.1, ...), custom_call_target="tpu_custom_call" | custom-call | flops 2100000000 | bytes 5000000 | tf_op jit(solution)/shard_map/pallas_call | solution.py:486
  90.8 1.9 %shard_map.112 = (bf16[80,192]{1,0:T(8,128)(2,1)}, bf16[640,128]{1,0:T(8,128)(2,1)}, bf16[640,128]{1,0:T(8,128)(2,1)}, bf16[128,640]{1,0:T(8,128)(2,1)}) custom-call(bf16[80,192]{1,0:T(8,128)(2,1)} %get-tuple-element.12.refs_0_, bf16[640,128]{1,0:T(8,128)(2,1)} %get-tuple-element.13.refs_1_, bf16[640,128]{1,0:T(8,128)(2,1)} %get-tuple-element.14.refs_2_, ...), custom_call_target="tpu_custom_call" | custom-call | tf_op jit(solution)/shard_map/pallas_call | solution.py:534
